TPU v7x, 32 devices: a whole 2x2x4 slice. The times are simulated.
32 devices in a mesh: dp: 8 (over y, x, core), mp: 4 (over z).
Axes of the slice: x: 2, y: 2, z: 4, core: 2. Of those that a mesh axis runs over, the one named last changes fastest.
Arguments:
- inputs: bfloat16 [16384, 1024], P(('dp', 'mp')), may hold values from -6 to 6
- lengths: int32 [16], replicated, may hold values from 0 to 4096, as said below
- attention_gain_one: bfloat16 [1024], P('dp'), may hold values from 0.25 to 1.75
- query_weight_one: bfloat16 [1024, 1024], P('dp', 'mp'), may hold values from -0.1875 to 0.1875
- key_weight_one: bfloat16 [1024, 1024], P('dp', 'mp'), may hold values from -0.1875 to 0.1875
- value_weight_one: bfloat16 [1024, 1024], P('dp', 'mp'), may hold values from -0.1875 to 0.1875
- output_weight_one: bfloat16 [1024, 1024], P('mp', 'dp'), may hold values from -1.5 to 1.5
- feedforward_gain_one: bfloat16 [1024], P('dp'), may hold values from 0.25 to 1.75
- gate_weight_one: bfloat16 [1024, 2816], P('dp', 'mp'), may hold values from -0.1875 to 0.1875
- up_weight_one: bfloat16 [1024, 2816], P('dp', 'mp'), may hold values from -0.1875 to 0.1875
- down_weight_one: bfloat16 [2816, 1024], P('mp', 'dp'), may hold values from -0.109375 to 0.109375
- attention_gain_two: bfloat16 [1024], P('dp'), may hold values from 0.25 to 1.75
- query_weight_two: bfloat16 [1024, 1024], P('dp', 'mp'), may hold values from -0.1875 to 0.1875
- key_weight_two: bfloat16 [1024, 1024], P('dp', 'mp'), may hold values from -0.1875 to 0.1875
- value_weight_two: bfloat16 [1024, 1024], P('dp', 'mp'), may hold values from -0.1875 to 0.1875
- output_weight_two: bfloat16 [1024, 1024], P('mp', 'dp'), may hold values from -1.5 to 1.5
- feedforward_gain_two: bfloat16 [1024], P('dp'), may hold values from 0.25 to 1.75
- gate_weight_two: bfloat16 [1024, 2816], P('dp', 'mp'), may hold values from -0.1875 to 0.1875
- up_weight_two: bfloat16 [1024, 2816], P('dp', 'mp'), may hold values from -0.1875 to 0.1875
- down_weight_two: bfloat16 [2816, 1024], P('mp', 'dp'), may hold values from -0.109375 to 0.109375
- cotangent: bfloat16 [16384, 1024], P(('dp', 'mp')), may hold values from -6 to 6
Outputs:
- first_output: bfloat16 [16384, 1024], P(('dp', 'mp'))
- second_output: bfloat16 [16384, 1024], P(('dp', 'mp'))
- input_grad: float32 [16384, 1024], P(('dp', 'mp'))
- grad_attention_gain_one: float32 [1024], P('dp')
- grad_query_one: float32 [1024, 1024], P('dp', 'mp')
- grad_key_one: float32 [1024, 1024], P('dp', 'mp')
- grad_value_one: float32 [1024, 1024], P('dp', 'mp')
- grad_output_one: float32 [1024, 1024], P('mp', 'dp')
- grad_feedforward_gain_one: float32 [1024], P('dp')
- grad_gate_one: float32 [1024, 2816], P('dp', 'mp')
- grad_up_one: float32 [1024, 2816], P('dp', 'mp')
- grad_down_one: float32 [2816, 1024], P('mp', 'dp')
- grad_attention_gain_two: float32 [1024], P('dp')
- grad_query_two: float32 [1024, 1024], P('dp', 'mp')
- grad_key_two: float32 [1024, 1024], P('dp', 'mp')
- grad_value_two: float32 [1024, 1024], P('dp', 'mp')
- grad_output_two: float32 [1024, 1024], P('mp', 'dp')
- grad_feedforward_gain_two: float32 [1024], P('dp')
- grad_gate_two: float32 [1024, 2816], P('dp', 'mp')
- grad_up_two: float32 [1024, 2816], P('dp', 'mp')
- grad_down_two: float32 [2816, 1024], P('mp', 'dp')
- value_norms: float32 [8, 2], P('dp')
Inputs may be any that keep to these rules, and one draw needn't show every extreme that they name: `lengths`: each entry is 0, 1024, 2048 or 4096; the entries sum to 16384; every 0 comes after all nonzero entries; some entry equals 4096.
All inputs are finite; a program needn't handle non-finite values.
Results may differ from a plain program's by a relative error of at most 0.035.
Values may be sent and summed in bfloat16 or wider, within the bound.
A program may use at most 384 MiB of HBM per device.

v0:
```python
import functools
import math

import jax
import jax.numpy as jnp
from jax import lax
from jax.experimental import pallas as pl
from jax.experimental.pallas import tpu as pltpu
from jax.sharding import PartitionSpec as P

D = 1024
HEAD_DIM = 64
TOK_DEV = 2048
LONGEST = 4096

LANES = 128
HEADS_HELD = LANES // HEAD_DIM
CHUNK = 1024
HALO = LONGEST - CHUNK
QUERY_ROWS = 1024
TILE = 256
EPSILON = 1e-06
MASKED = -1e30
LOG2E = math.log2(math.e)
MESH = pl.DeviceIdType.MESH
ANY = pl.BlockSpec(memory_space=pl.ANY)
VMEM = pl.BlockSpec(memory_space=pltpu.VMEM)
SMEM = pl.BlockSpec(memory_space=pltpu.SMEM)
BIG_VMEM = 56 * 1024 * 1024
BRIEF = pl.CostEstimate(flops=0, bytes_accessed=1_000, transcendentals=0)


def nn(left_side, right_side):
    return jnp.dot(left_side, right_side, preferred_element_type=jnp.float32)


def tn(left_side, right_side):
    return lax.dot_general(
        left_side, right_side, (((0,), (0,)), ((), ())), preferred_element_type=jnp.float32
    )


def nt(left_side, right_side):
    return lax.dot_general(
        left_side, right_side, (((1,), (1,)), ((), ())), preferred_element_type=jnp.float32
    )


def norm_rows(values, gain_vector):
    scaling = lax.rsqrt(jnp.mean(values * values, axis=-1, keepdims=True) + EPSILON)
    return values * scaling * gain_vector


def norm_back(values, gain_vector, grad_output):
    unused, pullback = jax.vjp(norm_rows, values, gain_vector)
    return pullback(grad_output)


class Plan:
    def __init__(self, n, m):
        self.n, self.m = n, m
        self.group = D // LANES
        self.low = self.group // m
        self.segments = n // self.low
        self.rows = TOK_DEV // m
        self.seg_rows = self.rows * self.group
        self.spans = []
        left, distance = HALO, 1
        while left > 0:
            count = min(self.seg_rows, left)
            self.spans.append((distance, left - count, count))
            left -= count
            distance += 1

    def here(self):
        dp, mp = lax.axis_index("dp"), lax.axis_index("mp")
        return dp // self.low, (dp % self.low) * self.m + mp

    def device(self, segment, member):
        return (segment * self.low + member // self.m, member % self.m)


def greet(plan, segment, member):
    barrier = pltpu.get_barrier_semaphore()
    for offset in range(1, plan.group):
        peer = lax.rem(member + offset, plan.group)
        pl.semaphore_signal(
            barrier, inc=1, device_id=plan.device(segment, peer), device_id_type=MESH
        )
    pl.semaphore_wait(barrier, plan.group - 1)


def member_copies(plan, segment, member, source, target, send, recv, own):
    copies = [pltpu.make_async_copy(source(member), target, own)]
    for offset in range(1, plan.group):
        peer = lax.rem(member + offset, plan.group)
        copies.append(
            pltpu.make_async_remote_copy(
                src_ref=source(peer),
                dst_ref=target,
                send_sem=send.at[offset],
                recv_sem=recv.at[offset],
                device_id=plan.device(segment, peer),
                device_id_type=MESH,
            )
        )
    for copy in copies[1:] + copies[:1]:
        copy.start()
    return copies


def columns(index):
    return pl.ds(pl.multiple_of(index * LANES, LANES), LANES)


def spread_kernel(plan, query, key, value, q_seg, k_seg, v_seg, send, recv, own):
    segment, member = plan.here()
    rows = plan.rows
    greet(plan, segment, member)
    copies = []
    place = pl.ds(pl.multiple_of(member * rows, rows), rows)
    for part, (array, out) in enumerate(((key, k_seg), (value, v_seg), (query, q_seg))):

        def source(peer, array=array):
            return array.at[:, columns(peer)]

        copies += member_copies(
            plan, segment, member, source, out.at[place], send.at[part], recv.at[part], own.at[part]
        )
    for copy in copies:
        copy.wait()


def spread(plan, query, key, value):
    segment = jax.ShapeDtypeStruct((plan.seg_rows, LANES), jnp.bfloat16)
    return pl.pallas_call(
        functools.partial(spread_kernel, plan),
        out_shape=(segment,) * 3,
        in_specs=[ANY] * 3,
        out_specs=(ANY, ANY, ANY),
        scratch_shapes=[
            pltpu.SemaphoreType.DMA((3, plan.group)),
            pltpu.SemaphoreType.DMA((3, plan.group)),
            pltpu.SemaphoreType.DMA((3,)),
        ],
        compiler_params=pltpu.CompilerParams(collective_id=1, has_side_effects=True),
        cost_estimate=BRIEF,
        name="spread",
    )(query, key, value)


def halo_of(plan, seg):
    parts = []
    for distance, first, count in reversed(plan.spans):
        route = [(i, i + distance * plan.low) for i in range(plan.n - distance * plan.low)]
        parts.append(lax.ppermute(seg[plan.seg_rows - count :], "dp", route))
    return parts[0] if len(parts) == 1 else jnp.concatenate(parts, axis=0)


def halo_back(plan, halo):
    parts = []
    for distance, first, count in plan.spans:
        route = [(i, i - distance * plan.low) for i in range(distance * plan.low, plan.n)]
        parts.append(lax.ppermute(halo[first : first + count], "dp", route))
    return parts


def to_rows_kernel(plan, seg, rows_out, send, recv, own):
    segment, member = plan.here()
    rows = plan.rows
    greet(plan, segment, member)

    def source(peer):
        return seg.at[pl.ds(pl.multiple_of(peer * rows, rows), rows)]

    for copy in member_copies(
        plan, segment, member, source, rows_out.at[:, columns(member)], send, recv, own
    ):
        copy.wait()


def to_rows(plan, seg):
    return pl.pallas_call(
        functools.partial(to_rows_kernel, plan),
        out_shape=jax.ShapeDtypeStruct((plan.rows, D), jnp.bfloat16),
        in_specs=[ANY],
        out_specs=ANY,
        scratch_shapes=[
            pltpu.SemaphoreType.DMA((plan.group,)),
            pltpu.SemaphoreType.DMA((plan.group,)),
            pltpu.SemaphoreType.DMA,
        ],
        compiler_params=pltpu.CompilerParams(collective_id=2, has_side_effects=True),
        cost_estimate=BRIEF,
        name="to_rows",
    )(seg)


def dp_place():
    dp = lax.axis_index("dp")
    return dp, dp % 2, (dp // 2) % 2, dp // 4


def greet_all(plan, dp, mp):
    barrier = pltpu.get_barrier_semaphore()
    others = [(dp, lax.rem(mp + k, plan.m)) for k in range(1, plan.m)]
    others += [(lax.rem(dp + k, plan.n), mp) for k in range(1, plan.n)]
    for other in others:
        pl.semaphore_signal(barrier, inc=1, device_id=other, device_id_type=MESH)
    pl.semaphore_wait(barrier, len(others))


def remote(source, target, send, recv, device):
    copy = pltpu.make_async_remote_copy(
        src_ref=source,
        dst_ref=target,
        send_sem=send,
        recv_sem=recv,
        device_id=device,
        device_id_type=MESH,
    )
    copy.start()
    return copy


def weave_kernel(plan, shard, gain, out, gain_out, own, *sems):
    z_send, z_recv, x_send, x_recv, y_send, y_recv, c_send, c_recv, g_send, g_recv = sems
    (dp, core, x, y), mp = dp_place(), lax.axis_index("mp")
    types, rows = shard.shape[:2]
    half = types // 2
    greet_all(plan, dp, mp)
    beside = dp + 1 - 2 * core
    dp_x, dp_y = dp + 2 - 4 * x, dp + 4 - 8 * y
    dp_xy = dp_x + 4 - 8 * y

    def block(index, column, first=0, count=types):
        z = lax.rem(mp + plan.m - index, plan.m)
        place = pl.ds(pl.multiple_of(z * rows, rows), rows)
        return out.at[pl.ds(first, count), place, columns(column)]

    def pass_on(index, column, sems, slot, device, first=0, count=types):
        region = block(index, column, first, count)
        return remote(
            region, region, sems[0].at[index, slot], sems[1].at[index, slot], (device, mp)
        )

    locals_ = [
        pltpu.make_async_copy(shard, block(0, dp), own.at[0]),
        pltpu.make_async_copy(gain, gain_out.at[:, columns(dp)], own.at[1]),
    ]
    for copy in locals_:
        copy.start()
    z_copies = [None]
    for k in range(1, plan.m):
        z_copies.append(
            remote(shard, block(0, dp), z_send.at[k], z_recv.at[k], (dp, lax.rem(mp + k, plan.m)))
        )
    copies = [
        remote(
            gain,
            gain_out.at[:, columns(dp)],
            g_send.at[k],
            g_recv.at[k],
            (lax.rem(dp + k, plan.n), mp),
        )
        for k in range(1, plan.n)
    ]
    x_sems, y_sems, c_sems = (x_send, x_recv), (y_send, y_recv), (c_send, c_recv)
    x_own, y_own, x_far, y_far, c_all = [], [], [], [], []

    def first_stage(index):
        if index == 0:
            for copy in locals_:
                copy.wait()
        else:
            z_copies[index].wait_recv()
        x_own.append(pass_on(index, dp, x_sems, 0, dp_x))
        y_own.append(pass_on(index, dp, y_sems, 0, dp_y))
        c_all.append(pass_on(index, dp, c_sems, 0, beside))

    def second_stage(index):
        x_own[index].wait_recv()
        y_far.append(pass_on(index, dp_x, y_sems, 1, dp_y, 0, half))
        c_all.append(pass_on(index, dp_x, c_sems, 1, beside))
        y_own[index].wait_recv()
        x_far.append(pass_on(index, dp_y, x_sems, 1, dp_x, half, types - half))
        c_all.append(pass_on(index, dp_y, c_sems, 2, beside))

    def third_stage(index):
        y_far[index].wait_recv()
        c_all.append(pass_on(index, dp_xy, c_sems, 3, beside, 0, half))
        x_far[index].wait_recv()
        c_all.append(pass_on(index, dp_xy, c_sems, 4, beside, half, types - half))

    for step in range(plan.m + 2):
        if step < plan.m:
            first_stage(step)
        if 1 <= step < plan.m + 1:
            second_stage(step - 1)
        if step >= 2:
            third_stage(step - 2)
    for copy in copies + c_all:
        copy.wait()
    for copy in z_copies[1:] + x_own + y_own + x_far + y_far:
        copy.wait_send()


def weave(plan, shard, gain):
    types, rows = shard.shape[:2]
    dma = pltpu.SemaphoreType.DMA
    return pl.pallas_call(
        functools.partial(weave_kernel, plan),
        in_specs=[ANY, ANY],
        out_specs=(ANY, ANY),
        out_shape=(
            jax.ShapeDtypeStruct((types, plan.m * rows, D), jnp.bfloat16),
            jax.ShapeDtypeStruct((gain.shape[0], D), jnp.bfloat16),
        ),
        scratch_shapes=[dma((2,))]
        + [dma((plan.m,))] * 2
        + [dma((plan.m, 2))] * 4
        + [dma((plan.m, 5))] * 2
        + [dma((plan.n,))] * 2,
        compiler_params=pltpu.CompilerParams(collective_id=6, has_side_effects=True),
        cost_estimate=BRIEF,
        name="weave",
    )(shard, gain)


def shed_kernel(plan, normed, dq, dk, dv, extra, out, left, parts, from_core, sums, *rest):
    from_first, sums_first, from_second, blocks, from_z, c_sems, f_sems, s_sems, z_sems = rest
    (dp, core, x, y), mp = dp_place(), lax.axis_index("mp")
    width = D // plan.n
    wide = D // 2
    greet_all(plan, dp, mp)
    beside, dp_x, dp_y = dp + 1 - 2 * core, dp + 2 - 4 * x, dp + 4 - 8 * y

    def rows_of(index):
        return pl.ds(pl.multiple_of(index * width, width), width)

    def plus(one, other):
        return (one.astype(jnp.float32) + other.astype(jnp.float32)).astype(jnp.bfloat16)

    left[...] = normed[...].T
    c_copies, first, second = [], [], []
    for half in range(2):
        for kind, array in enumerate((dq, dk, dv)):
            place = slice(kind * wide, (kind + 1) * wide)
            source = slice(half * wide, (half + 1) * wide)
            parts[half, :, place] = nn(left[...], array[:, source]).astype(jnp.bfloat16)
        parts[half, :, 3 * wide :] = extra[...].astype(jnp.bfloat16)
        c_copies.append(
            [
                remote(
                    parts.at[half, rows_of(2 * j + 1 - core)],
                    from_core.at[half, j],
                    c_sems.at[0, half, j],
                    c_sems.at[1, half, j],
                    (beside, mp),
                )
                for j in range(4)
            ]
        )
    for half in range(2):
        for j in range(4):
            c_copies[half][j].wait_recv()
            sums[half, j] = plus(parts[half, rows_of(2 * j + core), :], from_core[half, j])
        for k in range(2):
            away = 2 * k + 1 - x if half == 0 else 2 * (1 - y) + k
            first.append(
                remote(
                    sums.at[half, away],
                    from_first.at[half, k],
                    f_sems.at[0, half, k],
                    f_sems.at[1, half, k],
                    (dp_x if half == 0 else dp_y, mp),
                )
            )
    for half in range(2):
        for k in range(2):
            first[2 * half + k].wait_recv()
            kept = 2 * k + x if half == 0 else 2 * y + k
            sums_first[half, k] = plus(sums[half, kept], from_first[half, k])
        second.append(
            remote(
                sums_first.at[half, 1 - y if half == 0 else 1 - x],
                from_second.at[half],
                s_sems.at[0, half],
                s_sems.at[1, half],
                (dp_y if half == 0 else dp_x, mp),
            )
        )
    piece = D // plan.m
    for half in range(2):
        second[half].wait_recv()
        total = plus(sums_first[half, y if half == 0 else x], from_second[half])
        for member in range(2):
            index = 2 * half + member
            for kind in range(3):
                start = kind * wide + member * piece
                blocks[index, :, kind * piece : (kind + 1) * piece] = total[:, start : start + piece]
            blocks[index, :, 3 * piece :] = total[:, 3 * wide :]
    z_copies = []
    for k in range(1, plan.m):
        peer = lax.rem(mp + k, plan.m)
        z_copies.append(
            remote(
                blocks.at[peer], from_z.at[k], z_sems.at[0, k], z_sems.at[1, k], (dp, peer)
            )
        )
    result = blocks[mp].astype(jnp.float32)
    for k in range(1, plan.m):
        z_copies[k - 1].wait_recv()
        result = result + from_z[k].astype(jnp.float32)
    out[...] = result
    for copy in c_copies[0] + c_copies[1] + first + second + z_copies:
        copy.wait_send()


def shed(plan, normed, dqkv, extra):
    dma = pltpu.SemaphoreType.DMA
    width, wide, kept = D // plan.n, 3 * (D // 2) + LANES, 3 * (D // plan.m) + LANES

    def held(*shape):
        return pltpu.VMEM(shape, jnp.bfloat16)

    return pl.pallas_call(
        functools.partial(shed_kernel, plan),
        in_specs=[VMEM] * 5,
        out_specs=VMEM,
        out_shape=jax.ShapeDtypeStruct((width, kept), jnp.float32),
        scratch_shapes=[
            held(D, normed.shape[0]),
            held(2, D, wide),
            held(2, 4, width, wide),
            held(2, 4, width, wide),
            held(2, 2, width, wide),
            held(2, 2, width, wide),
            held(2, width, wide),
            held(plan.m, width, kept),
            held(plan.m, width, kept),
            dma((2, 2, 4)),
            dma((2, 2, 2)),
            dma((2, 2)),
            dma((2, plan.m)),
        ],
        compiler_params=pltpu.CompilerParams(
            collective_id=7, has_side_effects=True, vmem_limit_bytes=BIG_VMEM
        ),
        cost_estimate=BRIEF,
        name="shed",
    )(normed, *dqkv, extra)


def products_kernel(plan, sides, *refs):
    rows_in, refs = refs[0], refs[1:]
    lefts, rights = refs[: len(set(sides))], refs[len(set(sides)) : len(set(sides)) + len(sides)]
    seg, out, left_sides, tiles, send, recv, own, sent = refs[len(lefts) + len(rights) :]
    segment, member = plan.here()
    rows = plan.rows
    greet(plan, segment, member)

    def source(peer):
        return rows_in.at[:, columns(peer)]

    place = seg.at[pl.ds(pl.multiple_of(member * rows, rows), rows)]
    copies = member_copies(plan, segment, member, source, place, send, recv, own)
    for index, array in enumerate(lefts):
        left_sides[index] = array[...].T
    start, pending = 0, [None, None]
    slot = 0
    for array, side in zip(rights, sides):
        size = array.shape[1]
        width = size // 2 if size % (2 * LANES) == 0 and size > D else D
        for first in range(0, size, width):
            if pending[slot] is not None:
                pending[slot].wait()
            tiles[slot, :, :width] = nn(
                left_sides[side], array[:, first : first + width]
            ).astype(jnp.bfloat16)
            pending[slot] = pltpu.make_async_copy(
                tiles.at[slot, :, :width], out.at[:, pl.ds(start, width)], sent.at[slot]
            )
            pending[slot].start()
            start += width
            slot = 1 - slot
    for copy in pending + copies:
        copy.wait()


def products(plan, rows_in, lefts, rights, sides):
    rows, widest = lefts[0].shape[0], max(array.shape[1] for array in rights) // 2
    total = sum(array.shape[1] for array in rights)
    return pl.pallas_call(
        functools.partial(products_kernel, plan, sides),
        in_specs=[ANY] + [VMEM] * (len(lefts) + len(rights)),
        out_specs=(ANY, ANY),
        out_shape=(
            jax.ShapeDtypeStruct((plan.seg_rows, LANES), jnp.bfloat16),
            jax.ShapeDtypeStruct((D, total), jnp.bfloat16),
        ),
        scratch_shapes=[
            pltpu.VMEM((len(lefts), D, rows), jnp.bfloat16),
            pltpu.VMEM((2, D, widest), jnp.bfloat16),
            pltpu.SemaphoreType.DMA((plan.group,)),
            pltpu.SemaphoreType.DMA((plan.group,)),
            pltpu.SemaphoreType.DMA,
            pltpu.SemaphoreType.DMA((2,)),
        ],
        compiler_params=pltpu.CompilerParams(
            collective_id=len(lefts), has_side_effects=True, vmem_limit_bytes=BIG_VMEM
        ),
        cost_estimate=BRIEF,
        name="products",
    )(rows_in, *lefts, *rights)


def collect_kernel(plan, spans, more, *refs):
    parts = 1 if spans == 0 else 2
    arrays, halos, refs = refs[:parts], refs[parts : parts * (1 + spans)], refs[parts * (1 + spans) :]
    beside, refs = refs[:more], refs[more:]
    outs, refs = refs[:parts], refs[parts:]
    total, send, recv, own = refs[-4:]
    segment, member = plan.here()
    rows = plan.rows
    greet(plan, segment, member)
    copies = []
    for part, array in enumerate(arrays):
        if spans:
            for piece in range(plan.seg_rows // CHUNK):
                start = piece * CHUNK
                value = array[pl.ds(start, CHUNK), :]
                for index, (distance, first, count) in enumerate(plan.spans):
                    offset = start - (plan.seg_rows - count)
                    if offset >= 0:
                        halo = halos[part * spans + index][pl.ds(offset, CHUNK), :]
                        value = value + halo.astype(jnp.float32)
                total[part, pl.ds(start, CHUNK), :] = value.astype(jnp.bfloat16)
            array = total.at[part]

        def source(peer, array=array):
            return array.at[pl.ds(pl.multiple_of(peer * rows, rows), rows)]

        copies += member_copies(
            plan,
            segment,
            member,
            source,
            outs[part].at[:, columns(member)],
            send.at[part],
            recv.at[part],
            own.at[part],
        )
    if beside:
        (hidden, weights, middle), (final, down, loaded) = beside, refs[:3]
        load = pltpu.make_async_copy(weights.at[2], down, loaded)
        load.start()
        load.wait()
        for first in range(0, D, TILE):
            place = slice(first, first + TILE)
            final[:, place] = (middle[:, place] + nn(hidden[...], down[:, place])).astype(
                jnp.bfloat16
            )
    for copy in copies:
        copy.wait()


def collect(plan, arrays, halos, beside=()):
    parts, spans = len(arrays), len(plan.spans) if halos else 0
    return pl.pallas_call(
        functools.partial(collect_kernel, plan, spans, len(beside)),
        out_shape=(jax.ShapeDtypeStruct((plan.rows, D), jnp.bfloat16),) * (parts + bool(beside)),
        in_specs=[VMEM] * (parts + len(halos)) + [VMEM, ANY, VMEM][: len(beside)],
        out_specs=(ANY,) * parts + (VMEM,) * bool(beside),
        scratch_shapes=[pltpu.VMEM(one.shape[1:], one.dtype) for one in beside[1:2]]
        + [pltpu.SemaphoreType.DMA] * bool(beside)
        + [
            pltpu.VMEM((parts, plan.seg_rows if halos else 16, LANES), jnp.bfloat16),
            pltpu.SemaphoreType.DMA((parts, plan.group)),
            pltpu.SemaphoreType.DMA((parts, plan.group)),
            pltpu.SemaphoreType.DMA((parts,)),
        ],
        compiler_params=pltpu.CompilerParams(
            collective_id=5 if halos else 9 if beside else 8, has_side_effects=True, vmem_limit_bytes=BIG_VMEM
        ),
        cost_estimate=BRIEF,
        name="collect_kv" if halos else "collect_q",
    )(*arrays, *halos, *beside)


def swap_halves(values):
    lane = lax.broadcasted_iota(jnp.int32, values.shape, 1)
    half = HEAD_DIM // 2
    ahead = pltpu.roll(values, LANES - half, 1)
    behind = pltpu.roll(values, half, 1)
    return jnp.where(lax.rem(lane, HEAD_DIM) < half, ahead, behind)


def rotate(values, cosine, sine):
    return values * cosine + swap_halves(values) * sine


def of_head(values, head):
    lane = lax.broadcasted_iota(jnp.int32, values.shape, 1)
    return jnp.where(lane // HEAD_DIM == head, values, jnp.zeros_like(values))


def chunk_rows(index, size):
    return pl.ds(pl.multiple_of(index * size, size), size)


HALO_CHUNKS = HALO // CHUNK


def rotate_keys(prior, first, keys, cosine, sine, k_turned):
    def one(index, unused):
        table = chunk_rows(prior[first + index], CHUNK)
        rows = chunk_rows(index, CHUNK)
        k_turned[rows, :] = rotate(
            keys[rows, :].astype(jnp.float32), cosine[table, :], sine[table, :]
        ).astype(jnp.bfloat16)
        return unused

    lax.fori_loop(0, keys.shape[0] // CHUNK, one, 0)


def query_tables(prior, block, cosine, sine):
    rows = chunk_rows(prior[HALO_CHUNKS + block], QUERY_ROWS)
    return cosine[rows, :], sine[rows, :]


def turned_queries(prior, block, queries, cosine, sine):
    cos_rows, sin_rows = query_tables(prior, block, cosine, sine)
    turned = rotate(queries.astype(jnp.float32), cos_rows, sin_rows)
    return (turned * (LOG2E * HEAD_DIM ** (-0.5))).astype(jnp.bfloat16)


def by_head(parts):
    whole = parts[0]
    lane = lax.broadcasted_iota(jnp.int32, whole.shape, 1)
    for head in range(1, HEADS_HELD):
        whole = jnp.where(lane // HEAD_DIM == head, parts[head], whole)
    return whole


def needs_halo(prior, own_chunks):
    needed = prior[HALO_CHUNKS] > 0
    for chunk in range(1, min(own_chunks, HALO_CHUNKS)):
        needed = needed | (prior[HALO_CHUNKS + chunk] > chunk)
    return needed


ROW_PARTS = 4
UNITS = [(head, part) for part in range(ROW_PARTS) for head in range(HEADS_HELD)]


def add_keys(refs, first, diagonal):
    q_head, k_turned, v_wide, top, total = refs
    start_row = pl.multiple_of(first * CHUNK, CHUNK)
    part_rows = QUERY_ROWS // ROW_PARTS

    def queries(part):
        return slice(part * part_rows, (part + 1) * part_rows)

    def keys(part):
        return pl.ds(start_row, (part + 1) * part_rows if diagonal else CHUNK)

    def start(unit):
        head, part = unit
        return nt(q_head[head, queries(part), :], k_turned[keys(part), :])

    def finish(unit, scores):
        head, part = unit
        held = (head, queries(part))
        value_block = v_wide[keys(part), :]
        if diagonal:
            place = lax.broadcasted_iota(jnp.int32, scores.shape, 0) + part * part_rows
            other = lax.broadcasted_iota(jnp.int32, scores.shape, 1)
            scores = jnp.where(other <= place, scores, MASKED)
        highest = jnp.max(scores, axis=1, keepdims=True)
        if diagonal:
            weights = jnp.exp2((scores - highest).astype(jnp.bfloat16))
            total[held] = nn(weights, value_block)
            top[held] = jnp.broadcast_to(highest, (part_rows, LANES))
        else:
            before = top[held]
            after = jnp.maximum(before, highest)
            weights = jnp.exp2((scores - after[:, :1]).astype(jnp.bfloat16))
            shrink = jnp.exp2(before - after)
            shrink = jnp.concatenate([shrink, shrink], axis=1)
            total[held] = total[held] * shrink + nn(weights, value_block)
            top[held] = after

    scores = start(UNITS[0])
    for index, unit in enumerate(UNITS):
        following = start(UNITS[index + 1]) if index + 1 < len(UNITS) else None
        finish(unit, scores)
        scores = following


def mixed_of(total):
    return by_head([total[head, :, :LANES] / total[head, :, LANES:] for head in range(HEADS_HELD)])


def attend_own_kernel(
    prior, q_ref, keys, values, cosine, sine, out_ref, top_ref, sum_ref, *scratch
):
    k_turned, v_wide, q_head, top, total = scratch
    block = pl.program_id(0)

    @pl.when(block == 0)
    def _():
        rotate_keys(prior, HALO_CHUNKS, keys, cosine, sine, k_turned)
        v_wide[:, :LANES] = values[...]
        v_wide[:, LANES:] = jnp.ones((values.shape[0], LANES), jnp.bfloat16)

    turned = turned_queries(prior, block, q_ref[...], cosine, sine)
    for head in range(HEADS_HELD):
        q_head[head] = of_head(turned, head)
    held = (q_head, k_turned, v_wide, top, total)
    add_keys(held, block, True)

    def earlier_chunk(index, unused):
        add_keys(held, block - 1 - index, False)
        return unused

    lax.fori_loop(0, jnp.minimum(prior[HALO_CHUNKS + block], block), earlier_chunk, 0)
    out_ref[...] = mixed_of(total).astype(jnp.bfloat16)
    top_ref[...] = by_head([top[head] for head in range(HEADS_HELD)])
    sum_ref[...] = by_head([total[head, :, LANES:] for head in range(HEADS_HELD)])


def attend_own(prior, q_seg, keys, values, cosine, sine):
    seg_rows = q_seg.shape[0]
    query_spec = pl.BlockSpec((QUERY_ROWS, LANES), lambda i, prior: (i, 0))
    wide = jax.ShapeDtypeStruct((seg_rows, LANES), jnp.float32)
    return pl.pallas_call(
        attend_own_kernel,
        grid_spec=pltpu.PrefetchScalarGridSpec(
            num_scalar_prefetch=1,
            grid=(seg_rows // QUERY_ROWS,),
            in_specs=[query_spec, VMEM, VMEM, VMEM, VMEM],
            out_specs=(query_spec,) * 3,
            scratch_shapes=[
                pltpu.VMEM((seg_rows, LANES), jnp.bfloat16),
                pltpu.VMEM((seg_rows, 2 * LANES), jnp.bfloat16),
                pltpu.VMEM((HEADS_HELD, QUERY_ROWS, LANES), jnp.bfloat16),
                pltpu.VMEM((HEADS_HELD, QUERY_ROWS, LANES), jnp.float32),
                pltpu.VMEM((HEADS_HELD, QUERY_ROWS, 2 * LANES), jnp.float32),
            ],
        ),
        out_shape=(jax.ShapeDtypeStruct((seg_rows, LANES), jnp.bfloat16), wide, wide),
        compiler_params=pltpu.CompilerParams(vmem_limit_bytes=BIG_VMEM),
        cost_estimate=BRIEF,
        name="attend_own",
    )(prior, q_seg, keys, values, cosine, sine)


def copy_in(pairs, sems):
    copies = [
        pltpu.make_async_copy(source, target, sems.at[index])
        for index, (source, target) in enumerate(pairs)
    ]
    for copy in copies:
        copy.start()
    for copy in copies:
        copy.wait()


def attend_halo_kernel(
    own_chunks, prior, q_seg, keys, values, cos_hbm, sin_hbm, out_in, top_in, sum_in,
    out, top_out, sum_out, *scratch
):
    k_turned, v_wide, q_head, top, total, key_rows, value_rows, cosine, sine = scratch[:9]
    q_rows, out_rows, top_rows, sum_rows, sems = scratch[9:]

    def one_block(block, unused):
        count = prior[HALO_CHUNKS + block] - block
        rows = chunk_rows(block, QUERY_ROWS)

        @pl.when(count > 0)
        def _():
            turned = turned_queries(prior, block, q_rows[rows, :], cosine, sine)
            mixed, tops, sums = out_rows[rows, :], top_rows[rows, :], sum_rows[rows, :]
            for head in range(HEADS_HELD):
                lane = head * HEAD_DIM
                q_head[head] = of_head(turned, head)
                top[head] = jnp.broadcast_to(tops[:, lane : lane + 1], top.shape[1:])
                weight = jnp.broadcast_to(sums[:, lane : lane + 1], top.shape[1:])
                total[head, :, :LANES] = mixed.astype(jnp.float32) * weight
                total[head, :, LANES:] = weight

            def earlier_chunk(index, unused):
                held = (q_head, k_turned, v_wide, top, total)
                add_keys(held, HALO_CHUNKS - 1 - index, False)
                return unused

            lax.fori_loop(0, count, earlier_chunk, 0)
            out_rows[rows, :] = mixed_of(total).astype(jnp.bfloat16)
            top_rows[rows, :] = by_head([top[head] for head in range(HEADS_HELD)])
            sum_rows[rows, :] = by_head([total[head, :, LANES:] for head in range(HEADS_HELD)])

        return unused

    @pl.when(needs_halo(prior, own_chunks))
    def _():
        part = pl.ds(0, q_rows.shape[0])
        held = ((out, out_rows), (top_out, top_rows), (sum_out, sum_rows))
        copy_in(
            (
                (keys, key_rows), (values, value_rows), (cos_hbm, cosine), (sin_hbm, sine),
                (q_seg.at[part], q_rows), *((hbm.at[part], rows) for hbm, rows in held),
            ),
            sems,
        )
        rotate_keys(prior, 0, key_rows, cosine, sine, k_turned)
        v_wide[:, :LANES] = value_rows[...]
        v_wide[:, LANES:] = jnp.ones((value_rows.shape[0], LANES), jnp.bfloat16)
        lax.fori_loop(0, q_rows.shape[0] // QUERY_ROWS, one_block, 0)
        copy_in([(rows, hbm.at[part]) for hbm, rows in held], sems)


def attend_halo(prior, q_seg, keys, values, cosine, sine, earlier):
    part = (min(q_seg.shape[0], HALO), LANES)
    per_head = (HEADS_HELD, QUERY_ROWS, LANES)
    return pl.pallas_call(
        functools.partial(attend_halo_kernel, q_seg.shape[0] // CHUNK),
        in_specs=[SMEM] + [ANY] * 8,
        out_specs=(ANY,) * 3,
        out_shape=tuple(jax.ShapeDtypeStruct(one.shape, one.dtype) for one in earlier),
        scratch_shapes=[
            pltpu.VMEM((HALO, LANES), jnp.bfloat16),
            pltpu.VMEM((HALO, 2 * LANES), jnp.bfloat16),
            pltpu.VMEM(per_head, jnp.bfloat16),
            pltpu.VMEM(per_head, jnp.float32),
            pltpu.VMEM((HEADS_HELD, QUERY_ROWS, 2 * LANES), jnp.float32),
            pltpu.VMEM((HALO, LANES), jnp.bfloat16),
            pltpu.VMEM((HALO, LANES), jnp.bfloat16),
            pltpu.VMEM((LONGEST, LANES), jnp.float32),
            pltpu.VMEM((LONGEST, LANES), jnp.float32),
            pltpu.VMEM(part, jnp.bfloat16),
            pltpu.VMEM(part, jnp.bfloat16),
            pltpu.VMEM(part, jnp.float32),
            pltpu.VMEM(part, jnp.float32),
            pltpu.SemaphoreType.DMA((8,)),
        ],
        input_output_aliases={6: 0, 7: 1, 8: 2},
        compiler_params=pltpu.CompilerParams(vmem_limit_bytes=BIG_VMEM),
        cost_estimate=BRIEF,
        name="attend_halo",
    )(prior, q_seg, keys, values, cosine, sine, *earlier)


def prepare_back(refs, block, prior, queries, grads, mixed, tops, sums, cosine, sine):
    q_head, grad_head, row_stats = refs
    turned = turned_queries(prior, block, queries, cosine, sine)
    grads = grads.astype(jnp.float32) / sums
    dots = (grads * mixed.astype(jnp.float32)).T
    tops = tops.T
    grads = grads.astype(jnp.bfloat16)
    for head in range(HEADS_HELD):
        q_head[head] = of_head(turned, head)
        grad_head[head] = of_head(grads, head)
        lanes = slice(head * HEAD_DIM, (head + 1) * HEAD_DIM)
        row_stats[head, 0:1, :] = tops[head * HEAD_DIM : head * HEAD_DIM + 1, :]
        row_stats[head, 1:2, :] = jnp.sum(dots[lanes, :], axis=0, keepdims=True)


def add_keys_back(refs, first, diagonal):
    q_head, grad_head, row_stats, k_turned, values, dq_total, dk_total, dv_total = refs
    part_rows = QUERY_ROWS // ROW_PARTS

    def keys(part):
        start = pl.multiple_of(first * CHUNK + part * part_rows, part_rows)
        return pl.ds(start, part_rows)

    def queries(part):
        return slice(part * part_rows if diagonal else 0, QUERY_ROWS)

    def start(unit):
        head, part = unit
        rows, wanted = keys(part), queries(part)
        return (
            nt(k_turned[rows, :], q_head[head, wanted, :]),
            nt(values[rows, :], grad_head[head, wanted, :]),
        )

    def finish(unit, products_):
        head, part = unit
        rows, wanted = keys(part), queries(part)
        scores, grad_weights = products_
        weights = jnp.exp2((scores - row_stats[head, 0:1, wanted]).astype(jnp.bfloat16))
        if diagonal:
            other = lax.broadcasted_iota(jnp.int32, scores.shape, 0)
            place = lax.broadcasted_iota(jnp.int32, scores.shape, 1)
            weights = jnp.where(other <= place, weights, jnp.zeros_like(weights))
        grad_scores = weights * (grad_weights - row_stats[head, 1:2, wanted]).astype(jnp.bfloat16)
        dv_total[rows, :] += nn(weights, grad_head[head, wanted, :])
        dk_total[rows, :] += nn(grad_scores, q_head[head, wanted, :])
        dq_total[head, wanted, :] += tn(grad_scores, k_turned[rows, :])

    held = start(UNITS[0])
    for index, unit in enumerate(UNITS):
        following = start(UNITS[index + 1]) if index + 1 < len(UNITS) else None
        finish(unit, held)
        held = following


def turn_keys_back(prior, first_chunk, dk_total, dv_total, cosine, sine, dk_ref, dv_ref):
    def one(index, unused):
        table = chunk_rows(prior[first_chunk + index], CHUNK)
        rows = chunk_rows(index, CHUNK)
        turned = rotate(dk_total[rows, :], cosine[table, :], -sine[table, :]) * (1.0 / LOG2E)
        dk_ref[rows, :] = turned.astype(dk_ref.dtype)
        dv_ref[rows, :] = dv_total[rows, :].astype(dv_ref.dtype)
        return unused

    lax.fori_loop(0, dk_ref.shape[0] // CHUNK, one, 0)


def attend_back_own_kernel(
    prior, q_ref, grad_ref, out_ref, top_ref, sum_ref, keys, values, cosine, sine, dq_part,
    dq_ref, dk_ref, dv_ref, k_turned, q_head, grad_head, dq_total, dk_total, dv_total, row_stats
):
    block = pl.program_id(0)
    chunks_back = prior[HALO_CHUNKS + block]

    @pl.when(block == 0)
    def _():
        rotate_keys(prior, HALO_CHUNKS, keys, cosine, sine, k_turned)
        dk_total[...] = jnp.zeros_like(dk_total)
        dv_total[...] = jnp.zeros_like(dv_total)

    prepare_back(
        (q_head, grad_head, row_stats), block, prior, q_ref[...], grad_ref[...], out_ref[...],
        top_ref[...], sum_ref[...], cosine, sine,
    )
    from_halo = jnp.where(chunks_back > block, dq_part[...], jnp.zeros_like(dq_part))
    for head in range(HEADS_HELD):
        dq_total[head] = from_halo
    held = (q_head, grad_head, row_stats, k_turned, values, dq_total, dk_total, dv_total)
    add_keys_back(held, block, True)

    def whole(index, unused):
        add_keys_back(held, index, False)
        return unused

    lax.fori_loop(jnp.maximum(block - chunks_back, 0), block, whole, 0)
    cos_rows, sin_rows = query_tables(prior, block, cosine, sine)
    turned = rotate(by_head([dq_total[head] for head in range(HEADS_HELD)]), cos_rows, -sin_rows)
    dq_ref[...] = (turned * HEAD_DIM ** (-0.5)).astype(jnp.bfloat16)

    @pl.when(block == pl.num_programs(0) - 1)
    def _():
        turn_keys_back(prior, HALO_CHUNKS, dk_total, dv_total, cosine, sine, dk_ref, dv_ref)


def back_scratch(key_rows):
    per_head = (HEADS_HELD, QUERY_ROWS, LANES)
    return [
        pltpu.VMEM((key_rows, LANES), jnp.bfloat16),
        pltpu.VMEM(per_head, jnp.bfloat16),
        pltpu.VMEM(per_head, jnp.bfloat16),
        pltpu.VMEM(per_head, jnp.float32),
        pltpu.VMEM((key_rows, LANES), jnp.float32),
        pltpu.VMEM((key_rows, LANES), jnp.float32),
        pltpu.VMEM((HEADS_HELD, 8, QUERY_ROWS), jnp.float32),
    ]


def attend_back_own(prior, q_seg, grad_seg, seen, keys, values, cosine, sine, dq_part):
    seg_rows = q_seg.shape[0]
    query_spec = pl.BlockSpec((QUERY_ROWS, LANES), lambda i, prior: (i, 0))
    wide = jax.ShapeDtypeStruct((seg_rows, LANES), jnp.float32)
    return pl.pallas_call(
        attend_back_own_kernel,
        grid_spec=pltpu.PrefetchScalarGridSpec(
            num_scalar_prefetch=1,
            grid=(seg_rows // QUERY_ROWS,),
            in_specs=[query_spec] * 5 + [VMEM] * 4 + [query_spec],
            out_specs=(query_spec, VMEM, VMEM),
            scratch_shapes=back_scratch(seg_rows),
        ),
        out_shape=(jax.ShapeDtypeStruct((seg_rows, LANES), jnp.bfloat16), wide, wide),
        compiler_params=pltpu.CompilerParams(vmem_limit_bytes=BIG_VMEM),
        cost_estimate=BRIEF,
        name="attend_back_own",
    )(prior, q_seg, grad_seg, *seen, keys, values, cosine, sine, dq_part)


def attend_back_halo_kernel(
    own_chunks, prior, q_seg, grad_seg, mixed, tops, sums, keys, values, cos_hbm, sin_hbm,
    dq_out, dk_out, dv_out, *scratch
):
    k_turned, q_head, grad_head, dq_total, dk_total, dv_total, row_stats = scratch[:7]
    key_rows, value_rows, cosine, sine, dk_half, dv_half = scratch[7:13]
    q_rows, grad_rows, out_rows, top_rows, sum_rows, dq_rows, sems = scratch[13:]
    needed = needs_halo(prior, own_chunks)
    part = pl.ds(0, q_rows.shape[0])

    def one_block(block, unused):
        chunks_back = prior[HALO_CHUNKS + block]
        rows = chunk_rows(block, QUERY_ROWS)

        @pl.when(chunks_back > block)
        def _():
            prepare_back(
                (q_head, grad_head, row_stats), block, prior, q_rows[rows, :], grad_rows[rows, :],
                out_rows[rows, :], top_rows[rows, :], sum_rows[rows, :], cosine, sine,
            )
            dq_total[...] = jnp.zeros_like(dq_total)

            def whole(index, unused):
                add_keys_back(
                    (
                        q_head, grad_head, row_stats, k_turned, value_rows, dq_total, dk_total,
                        dv_total,
                    ),
                    index,
                    False,
                )
                return unused

            lax.fori_loop(HALO_CHUNKS + block - chunks_back, HALO_CHUNKS, whole, 0)
            dq_rows[rows, :] = by_head([dq_total[head] for head in range(HEADS_HELD)])

        return unused

    @pl.when(needed)
    def _():
        copy_in(
            (
                (keys, key_rows), (values, value_rows), (cos_hbm, cosine), (sin_hbm, sine),
                (q_seg.at[part], q_rows), (grad_seg.at[part], grad_rows),
                (mixed.at[part], out_rows), (tops.at[part], top_rows), (sums.at[part], sum_rows),
            ),
            sems,
        )
        rotate_keys(prior, 0, key_rows, cosine, sine, k_turned)
        dk_total[...] = jnp.zeros_like(dk_total)
        dv_total[...] = jnp.zeros_like(dv_total)
        lax.fori_loop(0, q_rows.shape[0] // QUERY_ROWS, one_block, 0)
        turn_keys_back(prior, 0, dk_total, dv_total, cosine, sine, dk_half, dv_half)
        copy_in(((dq_rows, dq_out.at[part]),), sems)

    @pl.when(jnp.logical_not(needed))
    def _():
        dk_half[...] = jnp.zeros_like(dk_half)
        dv_half[...] = jnp.zeros_like(dv_half)

    copy_in(((dk_half, dk_out), (dv_half, dv_out)), sems)


def attend_back_halo(prior, q_seg, grad_seg, seen, keys, values, cosine, sine):
    seg_rows = q_seg.shape[0]
    part = (min(seg_rows, HALO), LANES)
    half = jax.ShapeDtypeStruct((HALO, LANES), jnp.bfloat16)
    return pl.pallas_call(
        functools.partial(attend_back_halo_kernel, seg_rows // CHUNK),
        in_specs=[SMEM] + [ANY] * 9,
        out_specs=(ANY,) * 3,
        out_shape=(jax.ShapeDtypeStruct((seg_rows, LANES), jnp.float32), half, half),
        scratch_shapes=back_scratch(HALO)
        + [
            pltpu.VMEM((HALO, LANES), jnp.bfloat16),
            pltpu.VMEM((HALO, LANES), jnp.bfloat16),
            pltpu.VMEM((LONGEST, LANES), jnp.float32),
            pltpu.VMEM((LONGEST, LANES), jnp.float32),
            pltpu.VMEM((HALO, LANES), jnp.bfloat16),
            pltpu.VMEM((HALO, LANES), jnp.bfloat16),
            pltpu.VMEM(part, jnp.bfloat16),
            pltpu.VMEM(part, jnp.bfloat16),
            pltpu.VMEM(part, jnp.bfloat16),
            pltpu.VMEM(part, jnp.float32),
            pltpu.VMEM(part, jnp.float32),
            pltpu.VMEM(part, jnp.float32),
            pltpu.SemaphoreType.DMA((9,)),
        ],
        compiler_params=pltpu.CompilerParams(vmem_limit_bytes=BIG_VMEM),
        cost_estimate=BRIEF,
        name="attend_back_halo",
    )(prior, q_seg, grad_seg, *seen, keys, values, cosine, sine)


def attention(plan, tables, q_seg, k_seg, v_seg):
    k_halo, v_halo = halo_of(plan, k_seg), halo_of(plan, v_seg)
    earlier = attend_own(tables[0], q_seg, k_seg, v_seg, *tables[1:])
    seen = attend_halo(tables[0], q_seg, k_halo, v_halo, *tables[1:], earlier)
    return seen[0], (q_seg, k_seg, v_seg, k_halo, v_halo, seen)


def attention_back(plan, tables, kept, grad_seg, waiting, beside=()):
    q_seg, k_seg, v_seg, k_halo, v_halo, seen = kept
    queries = (tables[0], q_seg, grad_seg, seen)
    dq_part, dk_halo, dv_halo = attend_back_halo(*queries, k_halo, v_halo, *tables[1:])
    halos = halo_back(plan, dk_halo) + halo_back(plan, dv_halo)
    dq_part, waiting = lax.optimization_barrier((dq_part, waiting))
    dq, dk_own, dv_own = attend_back_own(*queries, k_seg, v_seg, *tables[1:], dq_part)
    dq, *final = collect(plan, (dq,), (), beside)
    dq, *halos = lax.optimization_barrier((dq, *halos))
    return (dq, *collect(plan, (dk_own, dv_own), halos)), waiting, *final


def rotary_tables():
    half = HEAD_DIM // 2
    lane = jnp.arange(LANES)
    frequency = jnp.exp(
        (lane % half).astype(jnp.float32) * (-2.0 * math.log(10000.0) / HEAD_DIM)
    )
    sign = jnp.where(lane % HEAD_DIM < half, -1.0, 1.0).astype(jnp.float32)
    step = 64
    fine = jnp.arange(step).astype(jnp.float32)[:, None] * frequency[None, :]
    coarse = jnp.arange(0, LONGEST, step).astype(jnp.float32)[:, None] * frequency[None, :]
    cos_fine, sin_fine, cos_coarse, sin_coarse = lax.optimization_barrier(
        (jnp.cos(fine), jnp.sin(fine), jnp.cos(coarse), jnp.sin(coarse))
    )
    cosine = cos_coarse[:, None] * cos_fine[None] - sin_coarse[:, None] * sin_fine[None]
    sine = sin_coarse[:, None] * cos_fine[None] + cos_coarse[:, None] * sin_fine[None]
    return (
        cosine.reshape(LONGEST, LANES),
        (sine * sign).reshape(LONGEST, LANES),
    )


def chunks_before(plan, lengths):
    segment, unused = plan.here()
    count = (HALO + plan.seg_rows) // CHUNK
    places = segment * plan.seg_rows - HALO + CHUNK * jnp.arange(count)
    ends = jnp.cumsum(lengths)
    passed = ends[None, :] <= places[:, None]
    opening = jnp.max(jnp.where(passed, ends[None, :], 0), axis=1)
    return jnp.clip((places - opening) // CHUNK, 0, HALO_CHUNKS).astype(jnp.int32)


def tied(array, *others):
    return lax.optimization_barrier((array, *others))[0]


def attention_pack(weights):
    return jnp.stack([weights[1].T, weights[2].T, weights[3].T, weights[4]])


def feedforward_pack(weights):
    return jnp.stack([weights[6].T, weights[7].T, weights[8]])


def fetch_mp(packs):
    rows = [pack.reshape(-1, pack.shape[-1]) for pack in packs]
    whole = rows[0] if len(rows) == 1 else jnp.concatenate(rows, axis=0)
    return lax.all_gather(whole, "mp", axis=0, tiled=False)


def fetch_dp(whole, first, pack):
    count, rows, width = pack.shape
    members = whole.shape[0]
    part = whole[:, first : first + count * rows].reshape(members, count, rows, width)
    part = part.transpose(1, 0, 2, 3).reshape(count, members * rows, width)
    return lax.all_gather(part, "dp", axis=2, tiled=True)


def turn_kernel(members, sizes, *refs):
    parts, out = refs[:-1], refs[-1]
    index, start, row = 0, 0, 0
    for size in sizes:
        if start == parts[index].shape[1]:
            index, start = index + 1, 0
        turned = parts[index][:, start : start + size].T
        count = size // members
        for member in range(members):
            out[member, row : row + count, :] = turned[member * count : (member + 1) * count, :]
        start += size
        row += count


def mp_blocks(plan, parts, sizes):
    rows = sum(sizes) // plan.m
    if parts[0].shape[0] == LANES:
        return pl.pallas_call(
            functools.partial(turn_kernel, plan.m, sizes),
            in_specs=[VMEM] * len(parts),
            out_specs=VMEM,
            out_shape=jax.ShapeDtypeStruct((plan.m, rows, LANES), jnp.bfloat16),
            compiler_params=pltpu.CompilerParams(vmem_limit_bytes=BIG_VMEM),
            cost_estimate=BRIEF,
            name="turn",
        )(*parts)
    turned, start, pieces = jnp.concatenate(parts, axis=1).T, 0, []
    for size in sizes:
        piece = turned[start : start + size]
        pieces.append(piece.reshape(plan.m, size // plan.m, turned.shape[1]))
        start += size
    return jnp.concatenate(pieces, axis=1)


def reduce_mp(plan, blocks, sizes):
    part = lax.psum_scatter(blocks, "mp", scatter_dimension=0, tiled=False).astype(jnp.float32)
    start, pieces = 0, []
    for size in sizes:
        pieces.append(part[start : start + size // plan.m])
        start += size // plan.m
    return pieces


def reduce_qkv(plan, gradient, extra):
    gradient = jnp.concatenate([gradient, extra.astype(jnp.bfloat16)], axis=1)
    part = lax.psum_scatter(gradient, "dp", scatter_dimension=0, tiled=True)
    width = D // plan.m
    blocks = part[:, : 3 * D].reshape(-1, 3, plan.m, width).transpose(2, 0, 1, 3)
    blocks = blocks.reshape(plan.m, -1, 3 * width)
    shared = jnp.broadcast_to(part[None, :, 3 * D :], (plan.m, part.shape[0], LANES))
    blocks = jnp.concatenate([blocks, shared], axis=2)
    return lax.psum_scatter(blocks, "mp", scatter_dimension=0, tiled=False).astype(jnp.float32)


def project(normed, attention, first_values):
    query, key, fresh = (nt(normed, attention[part]) for part in range(3))
    if first_values is not None:
        fresh = 0.5 * fresh + 0.5 * first_values.astype(jnp.float32)
    return tuple(array.astype(jnp.bfloat16) for array in (query, key, fresh))


def feed_forward(middle, gain, feedforward):
    normed_ff = norm_rows(middle, gain).astype(jnp.bfloat16)
    gate = nt(normed_ff, feedforward[0])
    upward = nt(normed_ff, feedforward[1])
    hidden = (jax.nn.silu(gate) * upward).astype(jnp.bfloat16)
    return normed_ff, gate, upward, hidden


def feed_forward_back(grad_final, middle, gain, weights, stored):
    attention, feedforward = weights
    normed_ff, gate, upward, hidden = stored
    grad_bar = grad_final.astype(jnp.bfloat16)
    grad_hidden = nt(grad_bar, feedforward[2])
    gate_sigmoid = jax.nn.sigmoid(gate)
    grad_gate = (
        grad_hidden * upward * gate_sigmoid * (1.0 + gate * (1.0 - gate_sigmoid))
    ).astype(jnp.bfloat16)
    grad_up = (grad_hidden * gate * gate_sigmoid).astype(jnp.bfloat16)
    grad_normed_ff = nn(grad_gate, feedforward[0]) + nn(grad_up, feedforward[1])
    grad_norm, grad_gain = norm_back(middle, gain, grad_normed_ff)
    grad_middle = grad_final + grad_norm
    middle_bar = grad_middle.astype(jnp.bfloat16)
    grad_mixed = nt(middle_bar, attention[3]).astype(jnp.bfloat16)
    return grad_middle, grad_gain, grad_mixed, (grad_bar, grad_gate, grad_up, middle_bar)


def project_back(grad_middle, stream, gain, attention, dqkv):
    grad_normed = sum(nn(array, attention[part]) for part, array in enumerate(dqkv))
    grad_norm, grad_gain = norm_back(stream, gain, grad_normed)
    return grad_middle + grad_norm, grad_gain


def square_sum(values):
    widened = values.astype(jnp.float32)
    return jnp.sum(widened * widened)


def shards(n, m, inputs, lengths, *rest):
    plan = Plan(n, m)
    first, second, cotangent = rest[:9], rest[9:18], rest[18]
    cosine, sine = rotary_tables()
    tables = (chunks_before(plan, lengths), cosine, sine)
    by_hand = (n, m) == (8, 4)
    gain_shard = jnp.stack([first[0], first[5], second[0], second[5]])
    attention_packs = attention_pack(first), attention_pack(second)
    feedforward_packs = feedforward_pack(first), feedforward_pack(second)
    feedforward_rows = feedforward_packs[0].shape[0] * feedforward_packs[0].shape[1]
    whole = fetch_mp(feedforward_packs)
    if by_hand:
        gain_shard = jnp.pad(gain_shard, ((0, 12), (0, 0)))
        attention_one, gains = weave(plan, attention_packs[0], gain_shard)
        whole = tied(whole, gains)
    else:
        gains = lax.all_gather(gain_shard, "dp", axis=1, tiled=True)
        attention_one = fetch_dp(fetch_mp(attention_packs[:1]), 0, attention_packs[0])
    feedforward_one = fetch_dp(whole, 0, feedforward_packs[0])
    gains = gains[:4].astype(jnp.float32)
    heads, hidden_rows = first[4].shape[0] * m, first[8].shape[0] * m
    rest_sizes = (hidden_rows, hidden_rows, hidden_rows, heads)

    stream = inputs.astype(jnp.float32)
    normed_one = norm_rows(stream, gains[0]).astype(jnp.bfloat16)
    qkv = project(normed_one, attention_one, None)
    values_one = qkv[2]
    q_seg, k_seg, v_seg = spread(plan, *qkv)
    feedforward_one, q_seg, pack_two = lax.optimization_barrier(
        (feedforward_one, q_seg, attention_packs[1])
    )
    whole_two = fetch_mp((pack_two,))
    out_seg, seen_one = attention(plan, tables, q_seg, k_seg, v_seg)
    out_seg, whole_two, whole = lax.optimization_barrier((out_seg, whole_two, whole))
    mixed_one = to_rows(plan, out_seg)
    attention_two = fetch_dp(whole_two, 0, pack_two)
    feedforward_two = fetch_dp(whole, feedforward_rows, feedforward_packs[1])
    middle_one = stream + nn(mixed_one, attention_one[3])
    ff_one = feed_forward(middle_one, gains[1], feedforward_one)
    between = middle_one + nn(ff_one[3], feedforward_one[2])

    normed_two = norm_rows(between, gains[2]).astype(jnp.bfloat16)
    qkv = project(normed_two, attention_two, values_one)
    values_two = qkv[2]
    q_seg, k_seg, v_seg = spread(plan, *qkv)
    out_seg, seen_two = attention(plan, tables, q_seg, k_seg, v_seg)
    mixed_two = to_rows(plan, out_seg)
    middle_two = between + nn(mixed_two, attention_two[3])
    ff_two = feed_forward(middle_two, gains[3], feedforward_two)

    grad_middle, gain_ff_two, grad_mixed, (bar, grad_gate, grad_up, middle_bar) = feed_forward_back(
        cotangent.astype(jnp.float32), middle_two, gains[3], (attention_two, feedforward_two), ff_two
    )
    grad_seg, rest = products(
        plan,
        grad_mixed,
        (bar, ff_two[0], middle_bar),
        (ff_two[3], grad_gate, grad_up, mixed_two),
        (0, 1, 1, 2),
    )
    rest_two = lax.psum_scatter(rest, "dp", scatter_dimension=0, tiled=True)
    dqkv, unused, final = attention_back(
        plan, tables, seen_two, grad_seg, (), (ff_two[3], feedforward_two, middle_two)
    )
    value_extra = 0.5 * dqkv[2].astype(jnp.float32)
    dqkv_two = (dqkv[0], dqkv[1], value_extra.astype(jnp.bfloat16))
    grad_between, gain_two = project_back(
        grad_middle, between, gains[2], attention_two, dqkv_two
    )

    qkv_two = jnp.concatenate(
        [tn(normed_two, array).astype(jnp.bfloat16) for array in dqkv_two], axis=1
    )
    grad_between, qkv_two = lax.optimization_barrier((grad_between, qkv_two))
    qkv_two = lax.psum_scatter(qkv_two, "dp", scatter_dimension=0, tiled=True)
    grad_middle, gain_ff_one, grad_mixed, (bar, grad_gate, grad_up, middle_bar) = feed_forward_back(
        grad_between, middle_one, gains[1], (attention_one, feedforward_one), ff_one
    )
    grad_mixed, rest_two = lax.optimization_barrier((grad_mixed, rest_two))
    grad_seg, rest = products(
        plan,
        grad_mixed,
        (bar, ff_one[0], middle_bar),
        (ff_one[3], grad_gate, grad_up, mixed_one),
        (0, 1, 1, 2),
    )
    rest_one = lax.psum_scatter(rest, "dp", scatter_dimension=0, tiled=True)
    dqkv, qkv_two = attention_back(plan, tables, seen_one, grad_seg, qkv_two)
    grad_values = dqkv[2].astype(jnp.float32) + value_extra
    dqkv_one = (dqkv[0], dqkv[1], grad_values.astype(jnp.bfloat16))
    input_grad, gain_one = project_back(grad_middle, stream, gains[0], attention_one, dqkv_one)
    input_grad, rest_one = lax.optimization_barrier((input_grad, rest_one))
    sizes = rest_sizes + (heads,) * 3 + rest_sizes
    blocks, dqkv_one = lax.optimization_barrier(
        (mp_blocks(plan, (rest_two, qkv_two, rest_one), sizes), dqkv_one)
    )
    reduced = reduce_mp(plan, blocks, sizes)
    down_two, gate_two, up_two, output_two, query_two, key_two, value_two = reduced[:7]
    down_one, gate_one, up_one, output_one = reduced[7:]
    squares = [square_sum(values_one), square_sum(values_two)]
    width = D // n
    own_row = jnp.arange(D) == lax.axis_index("dp") * width
    squares = [jnp.where(own_row, square, 0.0) for square in squares]
    extra = jnp.stack([gain_one, gain_ff_one, gain_two, gain_ff_two, *squares], axis=1)
    extra = jnp.pad(extra, ((0, 0), (0, LANES - extra.shape[1])))
    if by_hand:
        part = shed(plan, normed_one, dqkv_one, extra)
    else:
        whole = [tn(normed_one, array).astype(jnp.bfloat16) for array in dqkv_one]
        part = reduce_qkv(plan, jnp.concatenate(whole, axis=1), extra)
    piece = D // m
    query_one, key_one, value_one = (part[:, i * piece : (i + 1) * piece] for i in range(3))
    shared = part[:, 3 * piece :]
    value_norms = jnp.sqrt(shared[:1, 4:6] / (TOK_DEV * D))
    return (
        between.astype(jnp.bfloat16),
        final,
        input_grad,
        shared[:, 0], query_one, key_one, value_one, output_one,
        shared[:, 1], gate_one.T, up_one.T, down_one,
        shared[:, 2], query_two.T, key_two.T, value_two.T, output_two,
        shared[:, 3], gate_two.T, up_two.T, down_two,
        value_norms,
    )


def solution(mesh):
    tokens, row_split, column_split = P(("dp", "mp"), None), P("dp", "mp"), P("mp", "dp")
    layer = (
        P("dp"), row_split, row_split, row_split, column_split, P("dp"), row_split, row_split,
        column_split,
    )
    return jax.shard_map(
        functools.partial(shards, mesh.shape["dp"], mesh.shape["mp"]),
        mesh=mesh,
        in_specs=(tokens, P(), *layer, *layer, tokens),
        out_specs=(tokens, tokens, tokens, *layer, *layer, P("dp", None)),
        check_vma=False,
    )
```

profile of v0, /device:TPU:0, one launch (start us, length us, event | category | flops | bytes accessed | tf_op | source)
XLA Modules:
  0.0 1150.7 jit_solution(15120904837868471703)
XLA Ops:
  12.6 59.5 %weave.1 = (bf16[4,1024,1024]{2,1,0:T(8,128)(2,1)}, bf16[16,1024]{1,0:T(8,128)(2,1)}) custom-call(bf16[4,256,128]{2,1,0:T(8,128)(2,1)} %pad_maximum_fusion.4.shard, bf16[16,128]{1,0:T(8,128)(2,1)} %fusion.109.gain), custom_call_target="tpu_custom_call" | custom-call | bytes 1000 | tf_op jit(solution)/shard_map/weave/pallas_call | solution.py:311
  72.2 40.7 %all-gather.15.cloned.1.call-done = bf16[16896,128]{1,0:T(8,128)(2,1)} async-done(((bf16[4224,128]{1,0:T(8,128)(2,1)}), bf16[16896,128]{1,0:T(8,128)(2,1)}) %all-gather.15.cloned.1.call-update) | async-done | bytes 4325392 | tf_op jit(solution)/shard_map/all_gather | solution.py:1150
  119.3 4.3 fusion.90.key
  125.3 2.3 fusion.87.query
  127.6 2.9 fusion.34
  130.5 69.9 %spread.2 = (bf16[4096,128]{1,0:T(8,128)(2,1)}, bf16[4096,128]{1,0:T(8,128)(2,1)}, bf16[4096,128]{1,0:T(8,128)(2,1)}) custom-call(bf16[512,1024]{1,0:T(8,128)(2,1)} %fusion.87.query, bf16[512,1024]{1,0:T(8,128)(2,1)} %fusion.90.key, bf16[512,1024]{1,0:T(8,128)(2,1)} %get-tuple-element.334.value), custom_call_target="tpu_custom_call" | custom-call | bytes 1000 | tf_op jit(solution)/shard_map/spread/pallas_call | solution.py:136
  200.4 2.2 slice.194
  202.6 1.8 collective-permute-start
  205.4 3.4 collective-permute-start.1
  214.7 23.7 %attend_own.2 = (bf16[4096,128]{1,0:T(8,128)(2,1)}, f32[4096,128]{1,0:T(8,128)}, f32[4096,128]{1,0:T(8,128)}) custom-call(s32[7]{0:T(128)} %fusion.117.prior, bf16[4096,128]{1,0:T(8,128)(2,1)} %get-tuple-element.97.q_ref.q_seg, bf16[4096,128]{1,0:T(8,128)(2,1)} %get-tuple-element.98.keys, bf16[4096,128]{1,0:T(8,128)(2,1)} %get-tuple-element.99.values, ...), custom_call_target="tpu_custom_call" | custom-call | bytes 1000 | tf_op jit(solution)/shard_map/attend_own/pallas_call | solution.py:737
  240.5 2.3 copy.129
  246.4 25.9 %to_rows.2.refs_7_ = bf16[512,1024]{1,0:T(8,128)(2,1)} custom-call(bf16[4096,128]{1,0:T(8,128)(2,1)} %get-tuple-element.109.seg.mixed.out_ref), custom_call_target="tpu_custom_call" | custom-call | bytes 1000 | tf_op jit(solution)/shard_map/to_rows/pallas_call | solution.py:183
  272.3 3.5 multiply_reduce_fusion.9
  277.0 8.1 fusion.16
  285.1 9.2 multiply_convert_fusion.3
  294.4 3.2 multiply_reduce_fusion.8
  299.2 21.6 %all-gather.11.cloned.1.call-done = bf16[4,1024,1024]{2,1,0:T(8,128)(2,1)} async-done(((bf16[4,1024,128]{2,1,0:T(8,128)(2,1)}), bf16[4,1024,1024]{2,1,0:T(8,128)(2,1)}) %all-gather.11.cloned.1.call-update) | async-done | bytes 8388624 | tf_op jit(solution)/shard_map/all_gather | solution.py:1158
  320.9 4.0 fusion.85.key
  324.9 2.3 fusion.86.query
  327.2 2.9 multiply_reduce_fusion
  330.1 70.5 %spread.3 = (bf16[4096,128]{1,0:T(8,128)(2,1)}, bf16[4096,128]{1,0:T(8,128)(2,1)}, bf16[4096,128]{1,0:T(8,128)(2,1)}) custom-call(bf16[512,1024]{1,0:T(8,128)(2,1)} %fusion.86.query, bf16[512,1024]{1,0:T(8,128)(2,1)} %fusion.85.key, bf16[512,1024]{1,0:T(8,128)(2,1)} %get-tuple-element.336.value), custom_call_target="tpu_custom_call" | custom-call | bytes 1000 | tf_op jit(solution)/shard_map/spread/pallas_call | solution.py:136
  401.9 4.3 collective-permute-start.2
  406.3 4.5 collective-permute-start.3
  410.8 24.4 %attend_own.3 = (bf16[4096,128]{1,0:T(8,128)(2,1)}, f32[4096,128]{1,0:T(8,128)}, f32[4096,128]{1,0:T(8,128)}) custom-call(s32[7]{0:T(128)} %fusion.117.prior, bf16[4096,128]{1,0:T(8,128)(2,1)} %get-tuple-element.112.q_ref.q_seg, bf16[4096,128]{1,0:T(8,128)(2,1)} %get-tuple-element.114.keys, bf16[4096,128]{1,0:T(8,128)(2,1)} %get-tuple-element.115.values, ...), custom_call_target="tpu_custom_call" | custom-call | bytes 1000 | tf_op jit(solution)/shard_map/attend_own/pallas_call | solution.py:737
  435.2 8.4 collective-permute-done.3.values
  445.4 25.5 %to_rows.3.refs_7_ = bf16[512,1024]{1,0:T(8,128)(2,1)} custom-call(bf16[4096,128]{1,0:T(8,128)(2,1)} %get-tuple-element.119.seg.mixed.out_ref), custom_call_target="tpu_custom_call" | custom-call | bytes 1000 | tf_op jit(solution)/shard_map/to_rows/pallas_call | solution.py:183
  470.9 3.9 multiply_reduce_fusion.7
  476.3 9.2 fusion.21
  486.6 5.0 fusion
  491.6 10.8 multiply_convert_fusion.2
  502.4 5.2 fusion.18
  507.6 3.6 multiply_reduce_fusion.1
  512.6 4.3 fusion.84.refs_0_
  516.8 31.3 %products.2 = (bf16[4096,128]{1,0:T(8,128)(2,1)}, bf16[1024,9472]{1,0:T(8,128)(2,1)}) custom-call(bf16[512,1024]{1,0:T(8,128)(2,1)} %fusion.84.refs_0_, bf16[512,1024]{1,0:T(8,128)(2,1)} %refs_1_, bf16[512,1024]{1,0:T(8,128)(2,1)} %multiply_convert_fusion.4.refs_2_, bf16[512,1024]{1,0:T(8,128)(2,1)} %copy-done.21, ...), custom_call_target="tpu_custom_call" | custom-call | bytes 1000 | tf_op jit(solution)/shard_map/products/pallas_call | solution.py:494
  548.2 2.1 attend_back_halo.2
  553.0 39.3 %attend_back_own.2 = (bf16[4096,128]{1,0:T(8,128)(2,1)}, f32[4096,128]{1,0:T(8,128)}, f32[4096,128]{1,0:T(8,128)}) custom-call(s32[7]{0:T(128)} %fusion.117.prior, bf16[4096,128]{1,0:T(8,128)(2,1)} %get-tuple-element.112.q_ref.q_seg, bf16[4096,128]{1,0:T(8,128)(2,1)} %get-tuple-element.120.grad_seg.grad_ref, ...), custom_call_target="tpu_custom_call" | custom-call | bytes 1000 | tf_op jit(solution)/shard_map/attend_back_own/pallas_call | solution.py:975
  592.3 31.2 %collect_q.2 = (bf16[512,1024]{1,0:T(8,128)(2,1)}, bf16[512,1024]{1,0:T(8,128)(2,1)}) custom-call(bf16[4096,128]{1,0:T(8,128)(2,1)} %get-tuple-element.124.refs_0_, bf16[512,2816]{1,0:T(8,128)(2,1)} %get-tuple-element.290.refs_4_.refs_1_, bf16[3,2816,1024]{2,1,0:T(8,128)(2,1)} %all-gather.13.cloned.1.call-done.refs_2_, f32[512,1024]{1,0:T(8,128)} %copy-done), custom_call_target="tpu_custom_call" | custom-call | bytes 1000 | tf_op jit(solution)/shard_map/collect_q/pallas_call | solution.py:570
  623.5 14.1 %collective-permute-done.4.refs_2_ = bf16[3072,128]{1,0:T(8,128)(2,1)S(1)} collective-permute-done((bf16[3072,128]{1,0:T(8,128)(2,1)}, bf16[3072,128]{1,0:T(8,128)(2,1)S(1)}, u32[]{:S(2)}, u32[]{:S(2)}) %collective-permute-start.4) | collective-permute-done | bytes 786464 | tf_op jit(solution)/shard_map/ppermute | solution.py:164
  637.7 32.1 %collective-permute-done.5.refs_3_ = bf16[3072,128]{1,0:T(8,128)(2,1)S(1)} collective-permute-done((bf16[3072,128]{1,0:T(8,128)(2,1)}, bf16[3072,128]{1,0:T(8,128)(2,1)S(1)}, u32[]{:S(2)}, u32[]{:S(2)}) %collective-permute-start.5) | collective-permute-done | bytes 786464 | tf_op jit(solution)/shard_map/ppermute | solution.py:164
  670.7 53.5 %collect_kv.2 = (bf16[512,1024]{1,0:T(8,128)(2,1)}, bf16[512,1024]{1,0:T(8,128)(2,1)}) custom-call(f32[4096,128]{1,0:T(8,128)} %get-tuple-element.130.refs_0_, f32[4096,128]{1,0:T(8,128)} %get-tuple-element.131.refs_1_, bf16[3072,128]{1,0:T(8,128)(2,1)} %copy-done.40, bf16[3072,128]{1,0:T(8,128)(2,1)} %copy-done.42), custom_call_target="tpu_custom_call" | custom-call | bytes 1000 | tf_op jit(solution)/shard_map/collect_kv/pallas_call | solution.py:570
  724.2 3.3 fusion.60
  727.6 3.0 fusion.62
  730.7 4.8 multiply_reduce_fusion.2
  739.4 3.1 pad_maximum_fusion
  743.0 5.6 fusion.36
  750.4 9.8 multiply_convert_fusion.1
  760.2 7.3 fusion.10
  767.6 5.8 multiply_reduce_fusion.3
  773.4 1.9 fusion.121
  775.3 4.3 fusion.96.refs_0_
  779.5 31.1 %products.3 = (bf16[4096,128]{1,0:T(8,128)(2,1)}, bf16[1024,9472]{1,0:T(8,128)(2,1)}) custom-call(bf16[512,1024]{1,0:T(8,128)(2,1)} %fusion.96.refs_0_, bf16[512,1024]{1,0:T(8,128)(2,1)} %copy-done.19, bf16[512,1024]{1,0:T(8,128)(2,1)} %copy-done.20, bf16[512,1024]{1,0:T(8,128)(2,1)} %copy-done.22, bf16[512,2816]{1,0:T(8,128)(2,1)} %copy-done.27, ...), custom_call_target="tpu_custom_call" | custom-call | bytes 1000 | tf_op jit(solution)/shard_map/products/pallas_call | solution.py:494
  810.7 2.5 attend_back_halo.3
  815.8 24.9 %reduce-scatter.7.cloned.1.call-done.refs_1_ = bf16[128,3072]{1,0:T(8,128)(2,1)} async-done(((bf16[1024,3072]{1,0:T(8,128)(2,1)}), bf16[128,3072]{1,0:T(8,128)(2,1)}) %reduce-scatter.7.cloned.1.call-update) | async-done | bytes 786448 | tf_op jit(solution)/shard_map/reduce_scatter | solution.py:1333
  840.7 38.4 %attend_back_own.3 = (bf16[4096,128]{1,0:T(8,128)(2,1)}, f32[4096,128]{1,0:T(8,128)}, f32[4096,128]{1,0:T(8,128)}) custom-call(s32[7]{0:T(128)} %fusion.117.prior, bf16[4096,128]{1,0:T(8,128)(2,1)} %get-tuple-element.97.q_ref.q_seg, bf16[4096,128]{1,0:T(8,128)(2,1)} %get-tuple-element.139.grad_seg.grad_ref, ...), custom_call_target="tpu_custom_call" | custom-call | bytes 1000 | tf_op jit(solution)/shard_map/attend_back_own/pallas_call | solution.py:975
  879.1 26.2 %collect_q.3.dq = bf16[512,1024]{1,0:T(8,128)(2,1)} custom-call(bf16[4096,128]{1,0:T(8,128)(2,1)} %get-tuple-element.145.refs_0_), custom_call_target="tpu_custom_call" | custom-call | bytes 1000 | tf_op jit(solution)/shard_map/collect_q/pallas_call | solution.py:570
  906.5 52.1 %collect_kv.3 = (bf16[512,1024]{1,0:T(8,128)(2,1)}, bf16[512,1024]{1,0:T(8,128)(2,1)}) custom-call(f32[4096,128]{1,0:T(8,128)} %get-tuple-element.149.refs_0_, f32[4096,128]{1,0:T(8,128)} %get-tuple-element.150.refs_1_, bf16[3072,128]{1,0:T(8,128)(2,1)} %copy-done.39, bf16[3072,128]{1,0:T(8,128)(2,1)} %copy-done.41), custom_call_target="tpu_custom_call" | custom-call | bytes 1000 | tf_op jit(solution)/shard_map/collect_kv/pallas_call | solution.py:570
  960.4 3.2 fusion.49
  963.6 3.0 fusion.45
  966.7 3.6 fusion.31
  970.3 1.9 fusion.38
  972.1 7.1 reduce-scatter.9.cloned.1.call-done.refs_2_
  979.2 6.7 turn.1
  988.4 112.4 %shed.1 = f32[128,896]{1,0:T(8,128)} custom-call(bf16[512,1024]{1,0:T(8,128)(2,1)} %copy-done.17, bf16[512,1024]{1,0:T(8,128)(2,1)} %collect_q.3.dq, bf16[512,1024]{1,0:T(8,128)(2,1)} %get-tuple-element.161.dk, bf16[512,1024]{1,0:T(8,128)(2,1)} %copy-done.16, f32[1024,128]{1,0:T(8,128)} %pad.9.extra), custom_call_target="tpu_custom_call" | custom-call | bytes 1000 | tf_op jit(solution)/shard_map/shed/pallas_call | solution.py:427
  1105.7 31.4 %reduce-scatter.11.cloned.1.call-done = bf16[1,5504,128]{2,1,0:T(8,128)(2,1)} async-done(((bf16[4,5504,128]{2,1,0:T(8,128)(2,1)}), bf16[1,5504,128]{2,1,0:T(8,128)(2,1)}) %reduce-scatter.11.cloned.1.call-update) | async-done | bytes 1409040 | tf_op jit(solution)/shard_map/reduce_scatter | solution.py:1196
  (253 shorter events, 65.2 us)
Async XLA Ops:
  7.2 105.7 %all-gather.15.cloned.1.call-start = ((), (), s32[]{:S(2)}) async-start(), calls=%async_computation.12 | async-start | bytes 5406720 | tf_op jit(solution)/shard_map/all_gather | solution.py:1150
  10.8 199.9 %all-gather.7.cloned.1.call-start = ((), (), s32[]{:S(2)}) async-start(), calls=%async_computation.4 | async-start | bytes 19464192 | tf_op jit(solution)/shard_map/all_gather | solution.py:1158
  116.1 124.3 %all-gather.9.cloned.1.call-start = ((), (), s32[]{:S(2)}) async-start(), calls=%async_computation.5 | async-start | bytes 1310720 | tf_op jit(solution)/shard_map/all_gather | solution.py:1150
  118.2 5.4 copy-start.56
  118.9 4.7 copy-start.52
  119.0 157.4 %copy-start.54 = (f32[1,1024]{1,0:T(1,128)}, f32[1,1024]{1,0:T(1,128)S(1)}, u32[]{:S(2)}) copy-start(f32[1,1024]{1,0:T(1,128)S(1)} %get-tuple-element.313) | copy-start | bytes 12292
  119.3 8.3 copy-start.17
  119.3 6.0 copy-start.69
  200.3 4.1 copy-start.14
  200.4 8.4 copy-start.68
  200.4 8.6 copy-start.47
  200.4 8.7 copy-start.48
  200.4 8.8 copy-start.49
  200.4 9.2 copy-start.51
  202.6 35.8 %collective-permute-start = (bf16[3072,128]{1,0:T(8,128)(2,1)}, bf16[3072,128]{1,0:T(8,128)(2,1)S(1)}, u32[]{:S(2)}, u32[]{:S(2)}) collective-permute-start(bf16[3072,128]{1,0:T(8,128)(2,1)} %slice.194), channel_id=1, source_target_pairs={{0,8},{4,12},{8,16},{12,20},{16,24},{20,28},{1,9},{5,13},{9,17},{1... | collective-permute-start | bytes 2359304 | tf_op jit(solution)/shard_map/ppermute | solution.py:156
  205.4 33.0 %collective-permute-start.1 = (bf16[3072,128]{1,0:T(8,128)(2,1)}, bf16[3072,128]{1,0:T(8,128)(2,1)S(1)}, u32[]{:S(2)}, u32[]{:S(2)}) collective-permute-start(bf16[3072,128]{1,0:T(8,128)(2,1)} %slice.195), channel_id=1, source_target_pairs={{0,8},{4,12},{8,16},{12,20},{16,24},{20,28},{1,9},{5,13},{9,17},{1... | collective-permute-start | bytes 2359304 | tf_op jit(solution)/shard_map/ppermute | solution.py:156
  210.7 110.2 %all-gather.11.cloned.1.call-start = ((), (), s32[]{:S(2)}) async-start(), calls=%async_computation.6 | async-start | bytes 9437184 | tf_op jit(solution)/shard_map/all_gather | solution.py:1158
  242.8 233.5 %all-gather.13.cloned.1.call-start = ((), (), s32[]{:S(2)}) async-start(), calls=%async_computation.7 | async-start | bytes 19464192 | tf_op jit(solution)/shard_map/all_gather | solution.py:1158
  246.1 533.4 %reduce-scatter.5.cloned.1.call-start = ((), (), s32[]{:S(2)}) async-start(), calls=%async_computation.8 | async-start | bytes 21823488 | tf_op jit(solution)/shard_map/reduce_scatter | solution.py:1319
  275.8 18.6 %copy-start.10 = (f32[512,1024]{1,0:T(8,128)}, f32[512,1024]{1,0:T(8,128)S(1)}, u32[]{:S(2)}) copy-start(f32[512,1024]{1,0:T(8,128)S(1)} %get-tuple-element.322) | copy-start | bytes 6291460
  277.0 8.2 copy-start.20
  277.0 17.4 %slice-start = ((s8[17301504]{0:T(1024)(128)(4,1)}), s8[4194304]{0:T(1024)(128)(4,1)S(1)}, s32[]{:S(2)}) async-start(s8[17301504]{0:T(1024)(128)(4,1)} %bitcast.317), calls=%async_computation.13 | async-start | bytes 8388608
  277.0 17.4 %slice-start.1 = ((s8[17301504]{0:T(1024)(128)(4,1)}), s8[4194304]{0:T(1024)(128)(4,1)S(1)}, s32[]{:S(2)}) async-start(s8[17301504]{0:T(1024)(128)(4,1)} %bitcast.317), calls=%async_computation.14 | async-start | bytes 8388608
  285.1 9.2 slice-start.2
  285.1 9.2 slice-start.3
  285.1 9.3 slice-start.4
  294.3 3.3 copy-start.27
  299.2 27.9 %copy-start.37 = (bf16[512,1024]{1,0:T(8,128)(2,1)}, bf16[512,1024]{1,0:T(8,128)(2,1)S(1)}, u32[]{:S(2)}) copy-start(bf16[512,1024]{1,0:T(8,128)(2,1)S(1)} %multiply_convert_fusion.5) | copy-start | bytes 3145732
  320.9 4.0 copy-start.43
  400.6 5.6 copy-start.15
  401.9 33.3 %collective-permute-start.2 = (bf16[3072,128]{1,0:T(8,128)(2,1)S(1)}, bf16[3072,128]{1,0:T(8,128)(2,1)S(1)}, u32[]{:S(2)}, u32[]{:S(2)}) collective-permute-start(bf16[3072,128]{1,0:T(8,128)(2,1)S(1)} %slice.207), channel_id=1, source_target_pairs={{0,8},{4,12},{8,16},{12,20},{16,24},{20,28},{1,9},{5,13},{9,17},{1... | collective-permute-start | bytes 2359304 | tf_op jit(solution)/shard_map/ppermute | solution.py:156
  406.3 37.3 %collective-permute-start.3 = (bf16[3072,128]{1,0:T(8,128)(2,1)S(1)}, bf16[3072,128]{1,0:T(8,128)(2,1)S(1)}, u32[]{:S(2)}, u32[]{:S(2)}) collective-permute-start(bf16[3072,128]{1,0:T(8,128)(2,1)S(1)} %slice.208), channel_id=1, source_target_pairs={{0,8},{4,12},{8,16},{12,20},{16,24},{20,28},{1,9},{5,13},{9,17},{1... | collective-permute-start | bytes 2359304 | tf_op jit(solution)/shard_map/ppermute | solution.py:156
  435.2 8.4 copy-start.25
  474.8 36.4 %copy-start = (f32[512,1024]{1,0:T(8,128)}, f32[512,1024]{1,0:T(8,128)S(1)}, u32[]{:S(2)}) copy-start(f32[512,1024]{1,0:T(8,128)S(1)} %get-tuple-element.328.refs_3_) | copy-start | bytes 6291460
  476.3 9.2 copy-start.8
  476.3 10.3 copy-start.5
  502.4 5.2 copy-start.30
  512.6 4.3 copy-start.21
  548.2 292.5 %reduce-scatter.7.cloned.1.call-start = ((), (), s32[]{:S(2)}) async-start(), calls=%async_computation.9 | async-start | bytes 7077888 | tf_op jit(solution)/shard_map/reduce_scatter | solution.py:1333
  550.4 87.3 %collective-permute-start.4 = (bf16[3072,128]{1,0:T(8,128)(2,1)}, bf16[3072,128]{1,0:T(8,128)(2,1)S(1)}, u32[]{:S(2)}, u32[]{:S(2)}) collective-permute-start(bf16[3072,128]{1,0:T(8,128)(2,1)} %get-tuple-element.127), channel_id=1, source_target_pairs={{8,0},{12,4},{16,8},{20,12},{24,16},{28,20},{9,1},{13,5},{17,9},{2... | collective-permute-start | bytes 2359304 | tf_op jit(solution)/shard_map/ppermute | solution.py:164
  551.7 118.1 %collective-permute-start.5 = (bf16[3072,128]{1,0:T(8,128)(2,1)}, bf16[3072,128]{1,0:T(8,128)(2,1)S(1)}, u32[]{:S(2)}, u32[]{:S(2)}) collective-permute-start(bf16[3072,128]{1,0:T(8,128)(2,1)} %get-tuple-element.128), channel_id=1, source_target_pairs={{8,0},{12,4},{16,8},{20,12},{24,16},{28,20},{9,1},{13,5},{17,9},{2... | collective-permute-start | bytes 2359304 | tf_op jit(solution)/shard_map/ppermute | solution.py:164
  637.7 32.1 %copy-start.40 = (bf16[3072,128]{1,0:T(8,128)(2,1)}, bf16[3072,128]{1,0:T(8,128)(2,1)S(1)}, u32[]{:S(2)}) copy-start(bf16[3072,128]{1,0:T(8,128)(2,1)S(1)} %collective-permute-done.4.refs_2_) | copy-start | bytes 2359300
  724.2 3.3 copy-start.32
  727.6 3.1 copy-start.3
  727.6 3.1 copy-start.35
  730.6 4.8 copy-start.38
  739.4 3.1 copy-start.1
  739.4 3.6 copy-start.9
  748.7 230.5 %reduce-scatter.9.cloned.1.call-start = ((), (), s32[]{:S(2)}) async-start(), calls=%async_computation.10 | async-start | bytes 21823488 | tf_op jit(solution)/shard_map/reduce_scatter | solution.py:1345
  750.4 9.8 copy-start.19
  760.2 7.3 copy-start.29
  760.2 7.3 copy-start.28
  760.2 7.3 copy-start.11
  760.2 7.3 copy-start.55
  760.2 7.3 copy-start.61
  767.5 5.8 copy-start.63
  775.3 4.3 copy-start.22
  810.6 326.5 %reduce-scatter.11.cloned.1.call-start = ((), (), s32[]{:S(2)}) async-start(), calls=%async_computation.11 | async-start | bytes 7045120 | tf_op jit(solution)/shard_map/reduce_scatter | solution.py:1196
  813.2 92.1 %collective-permute-start.6 = (bf16[3072,128]{1,0:T(8,128)(2,1)}, bf16[3072,128]{1,0:T(8,128)(2,1)S(1)}, u32[]{:S(2)}, u32[]{:S(2)}) collective-permute-start(bf16[3072,128]{1,0:T(8,128)(2,1)} %get-tuple-element.146), channel_id=1, source_target_pairs={{8,0},{12,4},{16,8},{20,12},{24,16},{28,20},{9,1},{13,5},{17,9},{2... | collective-permute-start | bytes 2359304 | tf_op jit(solution)/shard_map/ppermute | solution.py:164
  814.5 90.9 %collective-permute-start.7 = (bf16[3072,128]{1,0:T(8,128)(2,1)}, bf16[3072,128]{1,0:T(8,128)(2,1)S(1)}, u32[]{:S(2)}, u32[]{:S(2)}) collective-permute-start(bf16[3072,128]{1,0:T(8,128)(2,1)} %get-tuple-element.147), channel_id=1, source_target_pairs={{8,0},{12,4},{16,8},{20,12},{24,16},{28,20},{9,1},{13,5},{17,9},{2... | collective-permute-start | bytes 2359304 | tf_op jit(solution)/shard_map/ppermute | solution.py:164
  906.5 52.1 %copy-start.33 = (bf16[512,1024]{1,0:T(8,128)(2,1)S(1)}, bf16[512,1024]{1,0:T(8,128)(2,1)}, u32[]{:S(2)}) copy-start(bf16[512,1024]{1,0:T(8,128)(2,1)} %get-tuple-element.135) | copy-start | bytes 3145732
  960.3 3.2 copy-start.16
  966.7 3.6 copy-start.59
  966.7 3.6 copy-start.13
  (29 other events, 55.3 us)
Sparse Core Ops, SparseCore 0:
  10.9 101.9 all-gather.14
  116.3 94.0 all-gather.6
  212.5 27.9 all-gather.8
  242.9 77.9 all-gather.10
  322.6 96.0 all-gather.12
  548.3 182.9 reduce-scatter.4
  748.8 91.8 reduce-scatter.6
  844.3 134.8 reduce-scatter.8
  986.0 151.0 reduce-scatter.10
where the time goes:
time: 1140 us; the launch traced here: 1150 us
  Pallas kernels  728 us (64%)
  waiting for transfers between devices  181 us (16%)
  matrix products  136 us (12%)
  local copies, waits for them, and re-layouts  37.8 us (3%)
  other arithmetic  32.4 us (3%)
  starting transfers between devices  20 us (2%)
  between operations  15.4 us (1%)
    pallas_call x4, Pallas kernels, collect(): pl.pallas_call(functools.partial(collect_kernel, plan, spans, len(beside)...  163 us
    pallas_call x2, Pallas kernels, spread(): pl.pallas_call(functools.partial(spread_kernel, plan), out_shape=(segment...  140 us
    pallas_call x1, Pallas kernels, shed(): pl.pallas_call(functools.partial(shed_kernel, plan), in_specs=[VMEM] * 5,...  112 us
    dot_general x14, matrix products, nt(): lax.dot_general(left_side, right_side, (((1,), (1,)), ((), ())), preferre...  79.2 us
    pallas_call x2, Pallas kernels, attend_back_own(): pl.pallas_call(attend_back_own_kernel, grid_spec=pltpu.PrefetchScalarGrid...  77.7 us
    pallas_call x2, Pallas kernels, products(): pl.pallas_call(functools.partial(products_kernel, plan, sides), in_specs=...  62.4 us
    pallas_call x1, Pallas kernels, weave(): pl.pallas_call(functools.partial(weave_kernel, plan), in_specs=[ANY, ANY]...  59.5 us
    dot_general x13, matrix products, nn(): return jnp.dot(left_side, right_side, preferred_element_type=jnp.float32)  53.3 us
  transfers between devices with their start and end apart: 17, of which 9 were waited for; matrix products, arithmetic and copies ran while one was open for 12% of the time, Pallas kernels for 60%

commit v1 on v0

--- a/solution.py
+++ b/solution.py
@@ -161,7 +161,7 @@
     parts = []
     for distance, first, count in plan.spans:
         route = [(i, i - distance * plan.low) for i in range(distance * plan.low, plan.n)]
-        parts.append(lax.ppermute(halo[first : first + count], "dp", route))
+        parts.append(lax.ppermute(halo[:, first : first + count], "dp", route))
     return parts
 
 
@@ -517,7 +517,7 @@
 
 def collect_kernel(plan, spans, more, *refs):
     parts = 1 if spans == 0 else 2
-    arrays, halos, refs = refs[:parts], refs[parts : parts * (1 + spans)], refs[parts * (1 + spans) :]
+    arrays, halos, refs = refs[:parts], refs[parts : parts + spans], refs[parts + spans :]
     beside, refs = refs[:more], refs[more:]
     outs, refs = refs[:parts], refs[parts:]
     total, send, recv, own = refs[-4:]
@@ -533,7 +533,7 @@
                 for index, (distance, first, count) in enumerate(plan.spans):
                     offset = start - (plan.seg_rows - count)
                     if offset >= 0:
-                        halo = halos[part * spans + index][pl.ds(offset, CHUNK), :]
+                        halo = halos[index][part, pl.ds(offset, CHUNK), :]
                         value = value + halo.astype(jnp.float32)
                 total[part, pl.ds(start, CHUNK), :] = value.astype(jnp.bfloat16)
             array = total.at[part]
@@ -990,7 +990,7 @@
 
 def attend_back_halo_kernel(
     own_chunks, prior, q_seg, grad_seg, mixed, tops, sums, keys, values, cos_hbm, sin_hbm,
-    dq_out, dk_out, dv_out, *scratch
+    dq_out, halves_out, *scratch
 ):
     k_turned, q_head, grad_head, dq_total, dk_total, dv_total, row_stats = scratch[:7]
     key_rows, value_rows, cosine, sine, dk_half, dv_half = scratch[7:13]
@@ -1048,18 +1048,20 @@
         dk_half[...] = jnp.zeros_like(dk_half)
         dv_half[...] = jnp.zeros_like(dv_half)
 
-    copy_in(((dk_half, dk_out), (dv_half, dv_out)), sems)
+    copy_in(((dk_half, halves_out.at[0]), (dv_half, halves_out.at[1])), sems)
 
 
 def attend_back_halo(prior, q_seg, grad_seg, seen, keys, values, cosine, sine):
     seg_rows = q_seg.shape[0]
     part = (min(seg_rows, HALO), LANES)
-    half = jax.ShapeDtypeStruct((HALO, LANES), jnp.bfloat16)
     return pl.pallas_call(
         functools.partial(attend_back_halo_kernel, seg_rows // CHUNK),
         in_specs=[SMEM] + [ANY] * 9,
-        out_specs=(ANY,) * 3,
-        out_shape=(jax.ShapeDtypeStruct((seg_rows, LANES), jnp.float32), half, half),
+        out_specs=(ANY,) * 2,
+        out_shape=(
+            jax.ShapeDtypeStruct((seg_rows, LANES), jnp.float32),
+            jax.ShapeDtypeStruct((2, HALO, LANES), jnp.bfloat16),
+        ),
         scratch_shapes=back_scratch(HALO)
         + [
             pltpu.VMEM((HALO, LANES), jnp.bfloat16),
@@ -1089,16 +1091,17 @@
     return seen[0], (q_seg, k_seg, v_seg, k_halo, v_halo, seen)
 
 
-def attention_back(plan, tables, kept, grad_seg, waiting, beside=()):
+def attention_back(plan, tables, kept, grad_seg, waiting, late, beside=()):
     q_seg, k_seg, v_seg, k_halo, v_halo, seen = kept
     queries = (tables[0], q_seg, grad_seg, seen)
-    dq_part, dk_halo, dv_halo = attend_back_halo(*queries, k_halo, v_halo, *tables[1:])
-    halos = halo_back(plan, dk_halo) + halo_back(plan, dv_halo)
+    dq_part, halves = attend_back_halo(*queries, k_halo, v_halo, *tables[1:])
+    halos = halo_back(plan, halves)
     dq_part, waiting = lax.optimization_barrier((dq_part, waiting))
     dq, dk_own, dv_own = attend_back_own(*queries, k_seg, v_seg, *tables[1:], dq_part)
     dq, *final = collect(plan, (dq,), (), beside)
     dq, *halos = lax.optimization_barrier((dq, *halos))
-    return (dq, *collect(plan, (dk_own, dv_own), halos)), waiting, *final
+    dkv, late = lax.optimization_barrier((collect(plan, (dk_own, dv_own), halos), late))
+    return (dq, *dkv), waiting, late, *final
 
 
 def rotary_tables():
@@ -1201,6 +1204,23 @@
     return pieces
 
 
+def reduce_mp_beside(plan, blocks, sizes):
+    me = lax.axis_index("mp")
+
+    def block(distance):
+        return lax.dynamic_index_in_dim(blocks, (me + distance) % plan.m, 0, keepdims=False)
+
+    total = block(0).astype(jnp.float32)
+    for distance in range(1, plan.m):
+        route = [(i, (i + distance) % plan.m) for i in range(plan.m)]
+        total = total + lax.ppermute(block(distance), "mp", route).astype(jnp.float32)
+    start, pieces = 0, []
+    for size in sizes:
+        pieces.append(total[start : start + size // plan.m])
+        start += size // plan.m
+    return pieces
+
+
 def reduce_qkv(plan, gradient, extra):
     gradient = jnp.concatenate([gradient, extra.astype(jnp.bfloat16)], axis=1)
     part = lax.psum_scatter(gradient, "dp", scatter_dimension=0, tiled=True)
@@ -1265,12 +1285,13 @@
     gain_shard = jnp.stack([first[0], first[5], second[0], second[5]])
     attention_packs = attention_pack(first), attention_pack(second)
     feedforward_packs = feedforward_pack(first), feedforward_pack(second)
-    feedforward_rows = feedforward_packs[0].shape[0] * feedforward_packs[0].shape[1]
-    whole = fetch_mp(feedforward_packs)
+    whole = fetch_mp(feedforward_packs[:1])
     if by_hand:
         gain_shard = jnp.pad(gain_shard, ((0, 12), (0, 0)))
         attention_one, gains = weave(plan, attention_packs[0], gain_shard)
+        whole, cosine, sine = lax.optimization_barrier((whole, cosine, sine))
         whole = tied(whole, gains)
+        tables = (tables[0], cosine, sine)
     else:
         gains = lax.all_gather(gain_shard, "dp", axis=1, tiled=True)
         attention_one = fetch_dp(fetch_mp(attention_packs[:1]), 0, attention_packs[0])
@@ -1284,15 +1305,16 @@
     qkv = project(normed_one, attention_one, None)
     values_one = qkv[2]
     q_seg, k_seg, v_seg = spread(plan, *qkv)
-    feedforward_one, q_seg, pack_two = lax.optimization_barrier(
-        (feedforward_one, q_seg, attention_packs[1])
-    )
-    whole_two = fetch_mp((pack_two,))
+    packs_two = (attention_packs[1], feedforward_packs[1])
+    feedforward_one, q_seg, packs_two = lax.optimization_barrier(
+        (feedforward_one, q_seg, packs_two)
+    )
+    whole_two = fetch_mp(packs_two)
     out_seg, seen_one = attention(plan, tables, q_seg, k_seg, v_seg)
-    out_seg, whole_two, whole = lax.optimization_barrier((out_seg, whole_two, whole))
+    out_seg, whole_two = lax.optimization_barrier((out_seg, whole_two))
     mixed_one = to_rows(plan, out_seg)
-    attention_two = fetch_dp(whole_two, 0, pack_two)
-    feedforward_two = fetch_dp(whole, feedforward_rows, feedforward_packs[1])
+    attention_two = fetch_dp(whole_two, 0, packs_two[0])
+    feedforward_two = fetch_dp(whole_two, 4 * packs_two[0].shape[1], packs_two[1])
     middle_one = stream + nn(mixed_one, attention_one[3])
     ff_one = feed_forward(middle_one, gains[1], feedforward_one)
     between = middle_one + nn(ff_one[3], feedforward_one[2])
@@ -1317,8 +1339,8 @@
         (0, 1, 1, 2),
     )
     rest_two = lax.psum_scatter(rest, "dp", scatter_dimension=0, tiled=True)
-    dqkv, unused, final = attention_back(
-        plan, tables, seen_two, grad_seg, (), (ff_two[3], feedforward_two, middle_two)
+    dqkv, unused, unused, final = attention_back(
+        plan, tables, seen_two, grad_seg, (), (), (ff_two[3], feedforward_two, middle_two)
     )
     value_extra = 0.5 * dqkv[2].astype(jnp.float32)
     dqkv_two = (dqkv[0], dqkv[1], value_extra.astype(jnp.bfloat16))
@@ -1342,19 +1364,26 @@
         (ff_one[3], grad_gate, grad_up, mixed_one),
         (0, 1, 1, 2),
     )
+    grad_seg, blocks, rest = lax.optimization_barrier(
+        (grad_seg, mp_blocks(plan, (tied(rest_two, grad_seg),), rest_sizes), rest)
+    )
+    reduced_two = reduce_mp_beside(plan, blocks, rest_sizes)
     rest_one = lax.psum_scatter(rest, "dp", scatter_dimension=0, tiled=True)
-    dqkv, qkv_two = attention_back(plan, tables, seen_one, grad_seg, qkv_two)
+    dqkv, qkv_two, reduced_two = attention_back(
+        plan, tables, seen_one, grad_seg, qkv_two, reduced_two
+    )
     grad_values = dqkv[2].astype(jnp.float32) + value_extra
     dqkv_one = (dqkv[0], dqkv[1], grad_values.astype(jnp.bfloat16))
     input_grad, gain_one = project_back(grad_middle, stream, gains[0], attention_one, dqkv_one)
     input_grad, rest_one = lax.optimization_barrier((input_grad, rest_one))
-    sizes = rest_sizes + (heads,) * 3 + rest_sizes
+    sizes = rest_sizes + (heads,) * 3
     blocks, dqkv_one = lax.optimization_barrier(
-        (mp_blocks(plan, (rest_two, qkv_two, rest_one), sizes), dqkv_one)
-    )
-    reduced = reduce_mp(plan, blocks, sizes)
-    down_two, gate_two, up_two, output_two, query_two, key_two, value_two = reduced[:7]
-    down_one, gate_one, up_one, output_one = reduced[7:]
+        (mp_blocks(plan, (rest_one, qkv_two), sizes), dqkv_one)
+    )
+    down_one, gate_one, up_one, output_one, query_two, key_two, value_two = reduce_mp(
+        plan, blocks, sizes
+    )
+    down_two, gate_two, up_two, output_two = reduced_two
     squares = [square_sum(values_one), square_sum(values_two)]
     width = D // n
     own_row = jnp.arange(D) == lax.axis_index("dp") * width

time: 1140 us -> 1100 us (0.965); the launches traced: 1150 us -> 1080 us
  waiting for transfers between devices: 181 us -> 109 us
    pallas_call x1, Pallas kernels: 112 us -> 78.5 us  [shed(): pl.pallas_call(functools.partial(shed_kernel, plan), in_specs=[VMEM] * 5,...]
    reduce_scatter x1, waiting for transfers between devices: 31.4 us -> 0.01 us  [reduce_mp(): lax.psum_scatter(blocks, 'mp', scatter_dimension=0, tiled=False)]
    reduce_scatter x1, waiting for transfers between devices: 24.9 us -> 0.02 us  [shards(): qkv_two = lax.psum_scatter(qkv_two, 'dp', scatter_dimension=0, tiled=True)]
    ppermute x4 -> x5, waiting for transfers between devices: 46.2 us -> 65.2 us  [the longest x2 65.2 us: halo_back(): parts.append(lax.ppermute(halo[:, first:first + count], 'dp', route))]
    all_gather x2, waiting for transfers between devices: 41 us -> 26.7 us  [fetch_mp(): return lax.all_gather(whole, 'mp', axis=0, tiled=False)]
    pallas_call x2, Pallas kernels: 140 us -> 154 us  [spread(): pl.pallas_call(functools.partial(spread_kernel, plan), out_shape=(segment...]
    all_gather x3, waiting for transfers between devices: 21.7 us -> 8.14 us  [fetch_dp(): return lax.all_gather(part, 'dp', axis=2, tiled=True)]
  transfers between devices with their start and end apart: 17 -> 18, of which waited for: 9 -> 7; matrix products, arithmetic and copies ran while one was open for 12% -> 14% of each run, Pallas kernels for 60% -> 63%
where the time goes in v1:
time: 1100 us; the launch traced here: 1080 us
  Pallas kernels  721 us (66%)
  matrix products  140 us (13%)
  waiting for transfers between devices  109 us (10%)
  local copies, waits for them, and re-layouts  40.2 us (4%)
  other arithmetic  34.4 us (3%)
  starting transfers between devices  22 us (2%)
  between operations  15.4 us (1%)
    pallas_call x4, Pallas kernels, collect(): pl.pallas_call(functools.partial(collect_kernel, plan, spans, len(beside)...  160 us
    pallas_call x2, Pallas kernels, spread(): pl.pallas_call(functools.partial(spread_kernel, plan), out_shape=(segment...  154 us
    pallas_call x2, Pallas kernels, attend_back_own(): pl.pallas_call(attend_back_own_kernel, grid_spec=pltpu.PrefetchScalarGrid...  88.7 us
    dot_general x14, matrix products, nt(): lax.dot_general(left_side, right_side, (((1,), (1,)), ((), ())), preferre...  82.8 us
    pallas_call x1, Pallas kernels, shed(): pl.pallas_call(functools.partial(shed_kernel, plan), in_specs=[VMEM] * 5,...  78.5 us
    ppermute x2, waiting for transfers between devices, halo_back(): parts.append(lax.ppermute(halo[:, first:first + count], 'dp', route))  65.2 us
    pallas_call x2, Pallas kernels, products(): pl.pallas_call(functools.partial(products_kernel, plan, sides), in_specs=...  62.1 us
    pallas_call x1, Pallas kernels, weave(): pl.pallas_call(functools.partial(weave_kernel, plan), in_specs=[ANY, ANY]...  59.8 us
  transfers between devices with their start and end apart: 18, of which 7 were waited for; matrix products, arithmetic and copies ran while one was open for 14% of the time, Pallas kernels for 63%

profile of v1, /device:TPU:0, one launch (start us, length us, event | category | flops | bytes accessed | tf_op | source)
XLA Modules:
  0.0 1082.6 jit_solution(13903549278633319568)
XLA Ops:
  7.3 2.0 pad_maximum_fusion.2
  13.9 59.8 %weave.1 = (bf16[4,1024,1024]{2,1,0:T(8,128)(2,1)}, bf16[16,1024]{1,0:T(8,128)(2,1)}) custom-call(bf16[4,256,128]{2,1,0:T(8,128)(2,1)} %pad_maximum_fusion.4.shard, bf16[16,128]{1,0:T(8,128)(2,1)} %fusion.111.gain), custom_call_target="tpu_custom_call" | custom-call | bytes 1000 | tf_op jit(solution)/shard_map/weave/pallas_call | solution.py:311
  77.0 2.4 all-gather.7.cloned.1.call-done
  79.3 3.1 copy.125
  85.7 4.2 fusion.87.query
  89.9 3.8 fusion.90.key
  93.8 4.5 fusion.34
  98.3 82.9 %spread.2 = (bf16[4096,128]{1,0:T(8,128)(2,1)}, bf16[4096,128]{1,0:T(8,128)(2,1)}, bf16[4096,128]{1,0:T(8,128)(2,1)}) custom-call(bf16[512,1024]{1,0:T(8,128)(2,1)} %fusion.87.query, bf16[512,1024]{1,0:T(8,128)(2,1)} %fusion.90.key, bf16[512,1024]{1,0:T(8,128)(2,1)} %get-tuple-element.354.value), custom_call_target="tpu_custom_call" | custom-call | bytes 1000 | tf_op jit(solution)/shard_map/spread/pallas_call | solution.py:136
  182.1 8.1 all-gather.9.cloned.1.call-done
  190.2 2.0 pad_maximum_fusion.1
  193.2 3.4 collective-permute-start
  197.6 2.4 collective-permute-start.1
  201.0 26.5 %attend_own.2 = (bf16[4096,128]{1,0:T(8,128)(2,1)}, f32[4096,128]{1,0:T(8,128)}, f32[4096,128]{1,0:T(8,128)}) custom-call(s32[7]{0:T(128)} %fusion.119.prior, bf16[4096,128]{1,0:T(8,128)(2,1)} %get-tuple-element.111.q_ref.q_seg, bf16[4096,128]{1,0:T(8,128)(2,1)} %get-tuple-element.112.keys, bf16[4096,128]{1,0:T(8,128)(2,1)} %get-tuple-element.113.values, ...), custom_call_target="tpu_custom_call" | custom-call | bytes 1000 | tf_op jit(solution)/shard_map/attend_own/pallas_call | solution.py:737
  227.5 3.5 collective-permute-done.1.values
  232.6 24.4 %all-gather.15.cloned.1.call-done = bf16[12544,128]{1,0:T(8,128)(2,1)} async-done(((bf16[3136,128]{1,0:T(8,128)(2,1)}), bf16[12544,128]{1,0:T(8,128)(2,1)}) %all-gather.15.cloned.1.call-update) | async-done | bytes 3211280 | tf_op jit(solution)/shard_map/all_gather | solution.py:1153
  262.9 24.7 %to_rows.2.refs_7_ = bf16[512,1024]{1,0:T(8,128)(2,1)} custom-call(bf16[4096,128]{1,0:T(8,128)(2,1)} %get-tuple-element.122.seg.mixed.out_ref), custom_call_target="tpu_custom_call" | custom-call | bytes 1000 | tf_op jit(solution)/shard_map/to_rows/pallas_call | solution.py:183
  287.6 3.4 multiply_reduce_fusion.9
  292.2 8.0 fusion.16
  300.3 9.2 multiply_convert_fusion.3
  309.5 3.2 multiply_reduce_fusion.8
  314.4 4.2 fusion.85.key
  319.0 2.3 fusion.86.query
  321.2 2.9 multiply_reduce_fusion
  324.2 71.3 %spread.3 = (bf16[4096,128]{1,0:T(8,128)(2,1)}, bf16[4096,128]{1,0:T(8,128)(2,1)}, bf16[4096,128]{1,0:T(8,128)(2,1)}) custom-call(bf16[512,1024]{1,0:T(8,128)(2,1)} %fusion.86.query, bf16[512,1024]{1,0:T(8,128)(2,1)} %fusion.85.key, bf16[512,1024]{1,0:T(8,128)(2,1)} %get-tuple-element.356.value), custom_call_target="tpu_custom_call" | custom-call | bytes 1000 | tf_op jit(solution)/shard_map/spread/pallas_call | solution.py:136
  396.8 3.4 collective-permute-start.2
  400.3 3.8 collective-permute-start.3
  404.1 27.2 %attend_own.3 = (bf16[4096,128]{1,0:T(8,128)(2,1)}, f32[4096,128]{1,0:T(8,128)}, f32[4096,128]{1,0:T(8,128)}) custom-call(s32[7]{0:T(128)} %fusion.119.prior, bf16[4096,128]{1,0:T(8,128)(2,1)} %get-tuple-element.125.q_ref.q_seg, bf16[4096,128]{1,0:T(8,128)(2,1)} %get-tuple-element.126.keys, bf16[4096,128]{1,0:T(8,128)(2,1)} %get-tuple-element.127.values, ...), custom_call_target="tpu_custom_call" | custom-call | bytes 1000 | tf_op jit(solution)/shard_map/attend_own/pallas_call | solution.py:737
  431.3 5.5 collective-permute-done.3.values
  438.6 25.5 %to_rows.3.refs_7_ = bf16[512,1024]{1,0:T(8,128)(2,1)} custom-call(bf16[4096,128]{1,0:T(8,128)(2,1)} %get-tuple-element.131.seg.mixed.out_ref), custom_call_target="tpu_custom_call" | custom-call | bytes 1000 | tf_op jit(solution)/shard_map/to_rows/pallas_call | solution.py:183
  464.1 3.9 multiply_reduce_fusion.7
  469.4 9.2 fusion.21
  479.7 5.0 fusion
  484.7 10.8 multiply_convert_fusion.2
  495.5 5.2 fusion.18
  500.7 3.6 multiply_reduce_fusion.1
  505.7 4.3 fusion.84.refs_0_
  510.0 31.3 %products.2 = (bf16[4096,128]{1,0:T(8,128)(2,1)}, bf16[1024,9472]{1,0:T(8,128)(2,1)}) custom-call(bf16[512,1024]{1,0:T(8,128)(2,1)} %fusion.84.refs_0_, bf16[512,1024]{1,0:T(8,128)(2,1)} %refs_1_, bf16[512,1024]{1,0:T(8,128)(2,1)} %multiply_convert_fusion.4.refs_2_, bf16[512,1024]{1,0:T(8,128)(2,1)} %copy-done.23, ...), custom_call_target="tpu_custom_call" | custom-call | bytes 1000 | tf_op jit(solution)/shard_map/products/pallas_call | solution.py:494
  541.4 2.1 attend_back_halo.2
  544.8 44.5 %attend_back_own.2 = (bf16[4096,128]{1,0:T(8,128)(2,1)}, f32[4096,128]{1,0:T(8,128)}, f32[4096,128]{1,0:T(8,128)}) custom-call(s32[7]{0:T(128)} %fusion.119.prior, bf16[4096,128]{1,0:T(8,128)(2,1)} %get-tuple-element.125.q_ref.q_seg, bf16[4096,128]{1,0:T(8,128)(2,1)} %get-tuple-element.132.grad_seg.grad_ref, ...), custom_call_target="tpu_custom_call" | custom-call | bytes 1000 | tf_op jit(solution)/shard_map/attend_back_own/pallas_call | solution.py:975
  589.3 30.0 %collect_q.2 = (bf16[512,1024]{1,0:T(8,128)(2,1)}, bf16[512,1024]{1,0:T(8,128)(2,1)}) custom-call(bf16[4096,128]{1,0:T(8,128)(2,1)} %get-tuple-element.136.refs_0_, bf16[512,2816]{1,0:T(8,128)(2,1)} %get-tuple-element.308.refs_4_.refs_1_, bf16[3,2816,1024]{2,1,0:T(8,128)(2,1)} %all-gather.13.cloned.1.call-done.refs_2_, f32[512,1024]{1,0:T(8,128)} %copy-done), custom_call_target="tpu_custom_call" | custom-call | bytes 1000 | tf_op jit(solution)/shard_map/collect_q/pallas_call | solution.py:570
  619.4 27.0 %collective-permute-done.4.refs_2_ = bf16[2,3072,128]{2,1,0:T(8,128)(2,1)S(1)} collective-permute-done((bf16[2,3072,128]{2,1,0:T(8,128)(2,1)}, bf16[2,3072,128]{2,1,0:T(8,128)(2,1)S(1)}, u32[]{:S(2)}, u32[]{:S(2)}) %collective-permute-start.4) | collective-permute-done | bytes 1572896 | tf_op jit(solution)/shard_map/ppermute | solution.py:164
  647.6 53.7 %collect_kv.2 = (bf16[512,1024]{1,0:T(8,128)(2,1)}, bf16[512,1024]{1,0:T(8,128)(2,1)}) custom-call(f32[4096,128]{1,0:T(8,128)} %get-tuple-element.141.refs_0_, f32[4096,128]{1,0:T(8,128)} %get-tuple-element.142.refs_1_, bf16[2,3072,128]{2,1,0:T(8,128)(2,1)} %copy-done.33), custom_call_target="tpu_custom_call" | custom-call | bytes 1000 | tf_op jit(solution)/shard_map/collect_kv/pallas_call | solution.py:570
  701.3 3.3 fusion.60
  704.6 3.0 fusion.62
  707.7 4.7 multiply_reduce_fusion.2
  716.4 3.1 pad_maximum_fusion
  720.0 5.7 fusion.36
  727.4 9.8 multiply_convert_fusion.1
  737.2 7.3 fusion.10
  744.6 6.2 multiply_reduce_fusion.3
  752.7 4.5 fusion.96.refs_0_
  757.2 30.8 %products.3 = (bf16[4096,128]{1,0:T(8,128)(2,1)}, bf16[1024,9472]{1,0:T(8,128)(2,1)}) custom-call(bf16[512,1024]{1,0:T(8,128)(2,1)} %fusion.96.refs_0_, bf16[512,1024]{1,0:T(8,128)(2,1)} %copy-done.21, bf16[512,1024]{1,0:T(8,128)(2,1)} %copy-done.22, bf16[512,1024]{1,0:T(8,128)(2,1)} %copy-done.24, bf16[512,2816]{1,0:T(8,128)(2,1)} %copy-done.29, ...), custom_call_target="tpu_custom_call" | custom-call | bytes 1000 | tf_op jit(solution)/shard_map/products/pallas_call | solution.py:494
  788.0 3.8 turn.2
  794.6 3.5 collective-permute-start.6
  800.5 2.5 attend_back_halo.3
  804.3 44.2 %attend_back_own.3 = (bf16[4096,128]{1,0:T(8,128)(2,1)}, f32[4096,128]{1,0:T(8,128)}, f32[4096,128]{1,0:T(8,128)}) custom-call(s32[7]{0:T(128)} %fusion.119.prior, bf16[4096,128]{1,0:T(8,128)(2,1)} %get-tuple-element.111.q_ref.q_seg, bf16[4096,128]{1,0:T(8,128)(2,1)} %get-tuple-element.153.grad_seg.grad_ref, ...), custom_call_target="tpu_custom_call" | custom-call | bytes 1000 | tf_op jit(solution)/shard_map/attend_back_own/pallas_call | solution.py:975
  848.5 25.6 %collect_q.3.dq = bf16[512,1024]{1,0:T(8,128)(2,1)} custom-call(bf16[4096,128]{1,0:T(8,128)(2,1)} %get-tuple-element.159.refs_0_), custom_call_target="tpu_custom_call" | custom-call | bytes 1000 | tf_op jit(solution)/shard_map/collect_q/pallas_call | solution.py:570
  877.5 38.2 %collective-permute-done.5.refs_2_ = bf16[2,3072,128]{2,1,0:T(8,128)(2,1)} collective-permute-done((bf16[2,3072,128]{2,1,0:T(8,128)(2,1)}, bf16[2,3072,128]{2,1,0:T(8,128)(2,1)}, u32[]{:S(2)}, u32[]{:S(2)}) %collective-permute-start.5) | collective-permute-done | bytes 1572896 | tf_op jit(solution)/shard_map/ppermute | solution.py:164
  915.7 50.2 %collect_kv.3 = (bf16[512,1024]{1,0:T(8,128)(2,1)}, bf16[512,1024]{1,0:T(8,128)(2,1)}) custom-call(f32[4096,128]{1,0:T(8,128)} %get-tuple-element.162.refs_0_, f32[4096,128]{1,0:T(8,128)} %get-tuple-element.163.refs_1_, bf16[2,3072,128]{2,1,0:T(8,128)(2,1)} %collective-permute-done.5.refs_2_), custom_call_target="tpu_custom_call" | custom-call | bytes 1000 | tf_op jit(solution)/shard_map/collect_kv/pallas_call | solution.py:570
  967.7 3.2 fusion.49
  971.0 3.0 fusion.45
  974.0 3.6 fusion.31
  979.5 4.4 turn.3
  986.3 78.5 %shed.1 = f32[128,896]{1,0:T(8,128)} custom-call(bf16[512,1024]{1,0:T(8,128)(2,1)} %copy-done.19, bf16[512,1024]{1,0:T(8,128)(2,1)} %collect_q.3.dq, bf16[512,1024]{1,0:T(8,128)(2,1)} %get-tuple-element.175.dk, bf16[512,1024]{1,0:T(8,128)(2,1)} %copy-done.18, f32[1024,128]{1,0:T(8,128)} %pad.9.extra), custom_call_target="tpu_custom_call" | custom-call | bytes 1000 | tf_op jit(solution)/shard_map/shed/pallas_call | solution.py:427
  (256 shorter events, 70.1 us)
Async XLA Ops:
  7.2 5.3 copy-start.66
  7.2 5.3 copy-start.65
  7.2 5.3 copy-start.64
  7.2 5.3 copy-start.63
  7.2 6.0 copy-start.49
  7.2 72.1 %all-gather.7.cloned.1.call-start = ((), (), s32[]{:S(2)}) async-start(), calls=%async_computation.4 | async-start | bytes 2703360 | tf_op jit(solution)/shard_map/all_gather | solution.py:1153
  9.3 180.9 %all-gather.9.cloned.1.call-start = ((), (), s32[]{:S(2)}) async-start(), calls=%async_computation.5 | async-start | bytes 19464192 | tf_op jit(solution)/shard_map/all_gather | solution.py:1161
  82.4 174.5 %all-gather.15.cloned.1.call-start = ((), (), s32[]{:S(2)}) async-start(), calls=%async_computation.12 | async-start | bytes 4014080 | tf_op jit(solution)/shard_map/all_gather | solution.py:1153
  84.6 5.3 copy-start.55
  85.3 4.6 copy-start.51
  85.4 206.3 %copy-start.53 = (f32[1,1024]{1,0:T(1,128)}, f32[1,1024]{1,0:T(1,128)S(1)}, u32[]{:S(2)}) copy-start(f32[1,1024]{1,0:T(1,128)S(1)} %get-tuple-element.333) | copy-start | bytes 12292
  85.7 8.1 copy-start.19
  98.3 82.9 %copy-start.50 = (bf16[256,128]{1,0:T(8,128)(2,1)S(1)}, bf16[256,128]{1,0:T(8,128)(2,1)}, u32[]{:S(2)}) copy-start(bf16[256,128]{1,0:T(8,128)(2,1)} %param.36) | copy-start | bytes 196612
  98.3 82.9 %copy-start.43 = (bf16[704,128]{1,0:T(8,128)(2,1)S(1)}, bf16[704,128]{1,0:T(8,128)(2,1)}, u32[]{:S(2)}) copy-start(bf16[704,128]{1,0:T(8,128)(2,1)} %param.40) | copy-start | bytes 540676
  98.3 83.0 %copy-start.44 = (bf16[128,704]{0,1:T(8,128)(2,1)S(1)}, bf16[128,704]{0,1:T(8,128)(2,1)}, u32[]{:S(2)}) copy-start(bf16[128,704]{0,1:T(8,128)(2,1)} %param.39) | copy-start | bytes 540676
  98.3 83.0 %copy-start.45 = (bf16[128,704]{0,1:T(8,128)(2,1)S(1)}, bf16[128,704]{0,1:T(8,128)(2,1)}, u32[]{:S(2)}) copy-start(bf16[128,704]{0,1:T(8,128)(2,1)} %param.38) | copy-start | bytes 540676
  181.1 11.1 %copy-start.15 = (bf16[4096,128]{1,0:T(8,128)(2,1)S(1)}, bf16[4096,128]{1,0:T(8,128)(2,1)}, u32[]{:S(2)}) copy-start(bf16[4096,128]{1,0:T(8,128)(2,1)} %get-tuple-element.112.keys) | copy-start | bytes 3145732
  182.1 14.6 %copy-start.16 = (bf16[4096,128]{1,0:T(8,128)(2,1)S(1)}, bf16[4096,128]{1,0:T(8,128)(2,1)}, u32[]{:S(2)}) copy-start(bf16[4096,128]{1,0:T(8,128)(2,1)} %get-tuple-element.113.values) | copy-start | bytes 3145732
  192.2 7.8 copy-start.67
  192.2 122.2 %all-gather.11.cloned.1.call-start = ((), (), s32[]{:S(2)}) async-start(), calls=%async_computation.6 | async-start | bytes 9437184 | tf_op jit(solution)/shard_map/all_gather | solution.py:1161
  193.2 34.2 %collective-permute-start = (bf16[3072,128]{1,0:T(8,128)(2,1)}, bf16[3072,128]{1,0:T(8,128)(2,1)S(1)}, u32[]{:S(2)}, u32[]{:S(2)}) collective-permute-start(bf16[3072,128]{1,0:T(8,128)(2,1)} %slice.181), channel_id=1, source_target_pairs={{0,8},{4,12},{8,16},{12,20},{16,24},{20,28},{1,9},{5,13},{9,17},{1... | collective-permute-start | bytes 2359304 | tf_op jit(solution)/shard_map/ppermute | solution.py:156
  197.6 33.4 %collective-permute-start.1 = (bf16[3072,128]{1,0:T(8,128)(2,1)}, bf16[3072,128]{1,0:T(8,128)(2,1)S(1)}, u32[]{:S(2)}, u32[]{:S(2)}) collective-permute-start(bf16[3072,128]{1,0:T(8,128)(2,1)} %slice.182), channel_id=1, source_target_pairs={{0,8},{4,12},{8,16},{12,20},{16,24},{20,28},{1,9},{5,13},{9,17},{1... | collective-permute-start | bytes 2359304 | tf_op jit(solution)/shard_map/ppermute | solution.py:156
  259.3 210.1 %all-gather.13.cloned.1.call-start = ((), (), s32[]{:S(2)}) async-start(), calls=%async_computation.7 | async-start | bytes 19464192 | tf_op jit(solution)/shard_map/all_gather | solution.py:1161
  262.7 494.5 %reduce-scatter.5.cloned.1.call-start = ((), (), s32[]{:S(2)}) async-start(), calls=%async_computation.8 | async-start | bytes 21823488 | tf_op jit(solution)/shard_map/reduce_scatter | solution.py:1341
  291.0 18.4 %copy-start.11 = (f32[512,1024]{1,0:T(8,128)}, f32[512,1024]{1,0:T(8,128)S(1)}, u32[]{:S(2)}) copy-start(f32[512,1024]{1,0:T(8,128)S(1)} %get-tuple-element.342) | copy-start | bytes 6291460
  292.2 8.1 copy-start.22
  292.2 17.2 %slice-start = ((s8[17301504]{0:T(1024)(128)(4,1)}), s8[4194304]{0:T(1024)(128)(4,1)S(1)}, s32[]{:S(2)}) async-start(s8[17301504]{0:T(1024)(128)(4,1)} %bitcast.318), calls=%async_computation.13 | async-start | bytes 8388608
  292.2 17.2 %slice-start.1 = ((s8[17301504]{0:T(1024)(128)(4,1)}), s8[4194304]{0:T(1024)(128)(4,1)S(1)}, s32[]{:S(2)}) async-start(s8[17301504]{0:T(1024)(128)(4,1)} %bitcast.318), calls=%async_computation.14 | async-start | bytes 8388608
  300.3 9.2 slice-start.2
  300.3 9.2 slice-start.3
  300.3 9.2 slice-start.4
  314.4 6.9 copy-start.40
  314.4 4.6 copy-start.42
  395.5 4.7 copy-start.17
  396.8 34.5 %collective-permute-start.2 = (bf16[3072,128]{1,0:T(8,128)(2,1)S(1)}, bf16[3072,128]{1,0:T(8,128)(2,1)S(1)}, u32[]{:S(2)}, u32[]{:S(2)}) collective-permute-start(bf16[3072,128]{1,0:T(8,128)(2,1)S(1)} %slice.195), channel_id=1, source_target_pairs={{0,8},{4,12},{8,16},{12,20},{16,24},{20,28},{1,9},{5,13},{9,17},{1... | collective-permute-start | bytes 2359304 | tf_op jit(solution)/shard_map/ppermute | solution.py:156
  400.3 36.5 %collective-permute-start.3 = (bf16[3072,128]{1,0:T(8,128)(2,1)S(1)}, bf16[3072,128]{1,0:T(8,128)(2,1)S(1)}, u32[]{:S(2)}, u32[]{:S(2)}) collective-permute-start(bf16[3072,128]{1,0:T(8,128)(2,1)S(1)} %slice.196), channel_id=1, source_target_pairs={{0,8},{4,12},{8,16},{12,20},{16,24},{20,28},{1,9},{5,13},{9,17},{1... | collective-permute-start | bytes 2359304 | tf_op jit(solution)/shard_map/ppermute | solution.py:156
  431.3 5.5 copy-start.27
  468.0 36.3 %copy-start = (f32[512,1024]{1,0:T(8,128)}, f32[512,1024]{1,0:T(8,128)S(1)}, u32[]{:S(2)}) copy-start(f32[512,1024]{1,0:T(8,128)S(1)} %get-tuple-element.348.refs_3_) | copy-start | bytes 6291460
  469.4 9.2 copy-start.9
  469.4 10.3 copy-start.5
  495.5 5.2 copy-start.32
  505.7 4.3 copy-start.23
  541.3 263.0 %reduce-scatter.7.cloned.1.call-start = ((), (), s32[]{:S(2)}) async-start(), calls=%async_computation.9 | async-start | bytes 7077888 | tf_op jit(solution)/shard_map/reduce_scatter | solution.py:1355
  543.5 102.9 %collective-permute-start.4 = (bf16[2,3072,128]{2,1,0:T(8,128)(2,1)}, bf16[2,3072,128]{2,1,0:T(8,128)(2,1)S(1)}, u32[]{:S(2)}, u32[]{:S(2)}) collective-permute-start(bf16[2,3072,128]{2,1,0:T(8,128)(2,1)} %get-tuple-element.139), channel_id=1, source_target_pairs={{8,0},{12,4},{16,8},{20,12},{24,16},{28,20},{9,1},{13,5},{17,9},{2... | collective-permute-start | bytes 4718600 | tf_op jit(solution)/shard_map/ppermute | solution.py:164
  707.7 4.8 copy-start.41
  716.4 3.6 copy-start.10
  725.7 253.8 %reduce-scatter.9.cloned.1.call-start = ((), (), s32[]{:S(2)}) async-start(), calls=%async_computation.10 | async-start | bytes 21823488 | tf_op jit(solution)/shard_map/reduce_scatter | solution.py:1371
  727.4 9.8 copy-start.21
  737.2 7.3 copy-start.31
  737.2 7.3 copy-start.30
  737.2 7.3 copy-start.12
  737.2 7.3 copy-start.54
  737.2 7.3 copy-start.60
  744.5 6.2 copy-start.62
  752.7 4.5 copy-start.24
  791.8 277.9 %reduce-scatter.11.cloned.1.call-start = ((), (), s32[]{:S(2)}) async-start(), calls=%async_computation.11 | async-start | bytes 4014080 | tf_op jit(solution)/shard_map/reduce_scatter | solution.py:1199
  794.6 79.5 %collective-permute-start.6 = (bf16[2368,128]{1,0:T(8,128)(2,1)}, bf16[2368,128]{1,0:T(8,128)(2,1)}, u32[]{:S(2)}, u32[]{:S(2)}) collective-permute-start(bf16[2368,128]{1,0:T(8,128)(2,1)} %get-tuple-element.311), channel_id=1, source_target_pairs={{0,1},{1,2},{2,3},{3,0},{4,5},{5,6},{6,7},{7,4},{8,9},{9,10},{10,1... | collective-permute-start | bytes 1818632 | tf_op jit(solution)/shard_map/ppermute | solution.py:1216
  798.1 76.0 %collective-permute-start.7 = (bf16[2368,128]{1,0:T(8,128)(2,1)}, bf16[2368,128]{1,0:T(8,128)(2,1)}, u32[]{:S(2)}, u32[]{:S(2)}) collective-permute-start(bf16[2368,128]{1,0:T(8,128)(2,1)} %get-tuple-element.313), channel_id=1, source_target_pairs={{0,2},{1,3},{2,0},{3,1},{4,6},{5,7},{6,4},{7,5},{8,10},{9,11},{10,... | collective-permute-start | bytes 1818632 | tf_op jit(solution)/shard_map/ppermute | solution.py:1216
  799.5 74.7 %collective-permute-start.8 = (bf16[2368,128]{1,0:T(8,128)(2,1)S(1)}, bf16[2368,128]{1,0:T(8,128)(2,1)}, u32[]{:S(2)}, u32[]{:S(2)}) collective-permute-start(bf16[2368,128]{1,0:T(8,128)(2,1)S(1)} %get-tuple-element.312), channel_id=1, source_target_pairs={{0,3},{1,0},{2,1},{3,2},{4,7},{5,4},{6,5},{7,6},{8,11},{9,8},{10,9... | collective-permute-start | bytes 1818632 | tf_op jit(solution)/shard_map/ppermute | solution.py:1216
  803.0 112.7 %collective-permute-start.5 = (bf16[2,3072,128]{2,1,0:T(8,128)(2,1)}, bf16[2,3072,128]{2,1,0:T(8,128)(2,1)}, u32[]{:S(2)}, u32[]{:S(2)}) collective-permute-start(bf16[2,3072,128]{2,1,0:T(8,128)(2,1)} %get-tuple-element.160), channel_id=1, source_target_pairs={{8,0},{12,4},{16,8},{20,12},{24,16},{28,20},{9,1},{13,5},{17,9},{2... | collective-permute-start | bytes 4718600 | tf_op jit(solution)/shard_map/ppermute | solution.py:164
  915.7 50.2 %copy-start.35 = (bf16[512,1024]{1,0:T(8,128)(2,1)S(1)}, bf16[512,1024]{1,0:T(8,128)(2,1)}, u32[]{:S(2)}) copy-start(bf16[512,1024]{1,0:T(8,128)(2,1)} %get-tuple-element.145) | copy-start | bytes 3145732
  974.0 3.6 copy-start.58
  974.0 3.6 copy-start.14
  1071.0 4.0 copy-start.39
  (28 other events, 55.5 us)
Sparse Core Ops, SparseCore 0:
  10.2 69.0 all-gather.6
  82.5 107.6 all-gather.8
  192.4 64.5 all-gather.14
  259.5 54.5 all-gather.10
  315.8 95.9 all-gather.12
  541.5 172.8 reduce-scatter.4
  725.8 76.5 reduce-scatter.6
  806.0 162.4 reduce-scatter.8
  984.0 81.2 reduce-scatter.10

commit v2 on v1

--- a/solution.py
+++ b/solution.py
@@ -1096,8 +1096,8 @@
     queries = (tables[0], q_seg, grad_seg, seen)
     dq_part, halves = attend_back_halo(*queries, k_halo, v_halo, *tables[1:])
     halos = halo_back(plan, halves)
-    dq_part, waiting = lax.optimization_barrier((dq_part, waiting))
     dq, dk_own, dv_own = attend_back_own(*queries, k_seg, v_seg, *tables[1:], dq_part)
+    dq, waiting = lax.optimization_barrier((dq, waiting))
     dq, *final = collect(plan, (dq,), (), beside)
     dq, *halos = lax.optimization_barrier((dq, *halos))
     dkv, late = lax.optimization_barrier((collect(plan, (dk_own, dv_own), halos), late))
@@ -1348,9 +1348,7 @@
         grad_middle, between, gains[2], attention_two, dqkv_two
     )
 
-    qkv_two = jnp.concatenate(
-        [tn(normed_two, array).astype(jnp.bfloat16) for array in dqkv_two], axis=1
-    )
+    qkv_two = tn(normed_two, jnp.concatenate(dqkv_two, axis=1)).astype(jnp.bfloat16)
     grad_between, qkv_two = lax.optimization_barrier((grad_between, qkv_two))
     qkv_two = lax.psum_scatter(qkv_two, "dp", scatter_dimension=0, tiled=True)
     grad_middle, gain_ff_one, grad_mixed, (bar, grad_gate, grad_up, middle_bar) = feed_forward_back(

time: 1100 us -> 1100 us (level)
  waiting for transfers between devices: 109 us -> 135 us
  Pallas kernels: 721 us -> 701 us
    pallas_call x2, Pallas kernels: 88.7 us -> 66.5 us  [attend_back_own(): pl.pallas_call(attend_back_own_kernel, grid_spec=pltpu.PrefetchScalarGrid...]
    ppermute x2, waiting for transfers between devices: 65.2 us -> 80 us  [halo_back(): parts.append(lax.ppermute(halo[:, first:first + count], 'dp', route))]
    ppermute x4, waiting for transfers between devices: 9 us -> 20.2 us  [halo_of(): parts.append(lax.ppermute(seg[plan.seg_rows - count:], 'dp', route))]
    pallas_call x2, Pallas kernels: 53.7 us -> 42.5 us  [attend_own(): pl.pallas_call(attend_own_kernel, grid_spec=pltpu.PrefetchScalarGridSpec(...]
  transfers between devices with their start and end apart: 18 -> 18, of which waited for: 7 -> 7; matrix products, arithmetic and copies ran while one was open for 14% -> 13% of each run, Pallas kernels for 63% -> 61%
where the time goes in v2:
time: 1100 us; the launch traced here: 1080 us
  Pallas kernels  701 us (64%)
  matrix products  140 us (13%)
  waiting for transfers between devices  135 us (12%)
  local copies, waits for them, and re-layouts  40.6 us (4%)
  other arithmetic  28.2 us (3%)
  starting transfers between devices  21.3 us (2%)
  between operations  15.4 us (1%)
    pallas_call x4, Pallas kernels, collect(): pl.pallas_call(functools.partial(collect_kernel, plan, spans, len(beside)...  170 us
    pallas_call x2, Pallas kernels, spread(): pl.pallas_call(functools.partial(spread_kernel, plan), out_shape=(segment...  154 us
    dot_general x14, matrix products, nt(): lax.dot_general(left_side, right_side, (((1,), (1,)), ((), ())), preferre...  82.5 us
    pallas_call x1, Pallas kernels, shed(): pl.pallas_call(functools.partial(shed_kernel, plan), in_specs=[VMEM] * 5,...  80.2 us
    ppermute x2, waiting for transfers between devices, halo_back(): parts.append(lax.ppermute(halo[:, first:first + count], 'dp', route))  80 us
    pallas_call x2, Pallas kernels, attend_back_own(): pl.pallas_call(attend_back_own_kernel, grid_spec=pltpu.PrefetchScalarGrid...  66.5 us
    pallas_call x2, Pallas kernels, products(): pl.pallas_call(functools.partial(products_kernel, plan, sides), in_specs=...  62.6 us
    pallas_call x1, Pallas kernels, weave(): pl.pallas_call(functools.partial(weave_kernel, plan), in_specs=[ANY, ANY]...  59.8 us
  transfers between devices with their start and end apart: 18, of which 7 were waited for; matrix products, arithmetic and copies ran while one was open for 13% of the time, Pallas kernels for 61%

profile of v2, /device:TPU:0, one launch (start us, length us, event | category | flops | bytes accessed | tf_op | source)
XLA Modules:
  0.0 1081.9 jit_solution(13427766320020550339)
XLA Ops:
  13.9 59.8 %weave.1 = (bf16[4,1024,1024]{2,1,0:T(8,128)(2,1)}, bf16[16,1024]{1,0:T(8,128)(2,1)}) custom-call(bf16[4,256,128]{2,1,0:T(8,128)(2,1)} %pad_maximum_fusion.3.shard, bf16[16,128]{1,0:T(8,128)(2,1)} %fusion.114.gain), custom_call_target="tpu_custom_call" | custom-call | bytes 1000 | tf_op jit(solution)/shard_map/weave/pallas_call | solution.py:311
  76.9 2.4 all-gather.7.cloned.1.call-done
  79.3 3.1 copy.113
  85.7 4.2 fusion.92.query
  89.9 3.8 fusion.95.key
  93.8 4.5 fusion.39
  98.2 82.9 %spread.2 = (bf16[4096,128]{1,0:T(8,128)(2,1)}, bf16[4096,128]{1,0:T(8,128)(2,1)}, bf16[4096,128]{1,0:T(8,128)(2,1)}) custom-call(bf16[512,1024]{1,0:T(8,128)(2,1)} %fusion.92.query, bf16[512,1024]{1,0:T(8,128)(2,1)} %fusion.95.key, bf16[512,1024]{1,0:T(8,128)(2,1)} %get-tuple-element.354.value), custom_call_target="tpu_custom_call" | custom-call | bytes 1000 | tf_op jit(solution)/shard_map/spread/pallas_call | solution.py:136
  182.1 8.1 all-gather.9.cloned.1.call-done
  190.2 2.0 pad_maximum_fusion
  193.2 3.4 collective-permute-start
  197.6 2.4 collective-permute-start.1
  200.9 20.9 %attend_own.2 = (bf16[4096,128]{1,0:T(8,128)(2,1)}, f32[4096,128]{1,0:T(8,128)}, f32[4096,128]{1,0:T(8,128)}) custom-call(s32[7]{0:T(128)} %fusion.122.prior, bf16[4096,128]{1,0:T(8,128)(2,1)} %get-tuple-element.111.q_ref.q_seg, bf16[4096,128]{1,0:T(8,128)(2,1)} %get-tuple-element.112.keys, bf16[4096,128]{1,0:T(8,128)(2,1)} %get-tuple-element.113.values, ...), custom_call_target="tpu_custom_call" | custom-call | bytes 1000 | tf_op jit(solution)/shard_map/attend_own/pallas_call | solution.py:737
  221.8 9.1 collective-permute-done.1.values
  232.6 24.4 %all-gather.15.cloned.1.call-done = bf16[12544,128]{1,0:T(8,128)(2,1)} async-done(((bf16[3136,128]{1,0:T(8,128)(2,1)}), bf16[12544,128]{1,0:T(8,128)(2,1)}) %all-gather.15.cloned.1.call-update) | async-done | bytes 3211280 | tf_op jit(solution)/shard_map/all_gather | solution.py:1153
  262.9 24.7 %to_rows.2.refs_7_ = bf16[512,1024]{1,0:T(8,128)(2,1)} custom-call(bf16[4096,128]{1,0:T(8,128)(2,1)} %get-tuple-element.122.seg.mixed.out_ref), custom_call_target="tpu_custom_call" | custom-call | bytes 1000 | tf_op jit(solution)/shard_map/to_rows/pallas_call | solution.py:183
  287.6 3.4 multiply_reduce_fusion.9
  292.2 8.0 fusion.16
  300.2 9.2 multiply_convert_fusion.3
  309.5 3.2 multiply_reduce_fusion.8
  314.4 4.2 fusion.90.key
  318.9 2.3 fusion.91.query
  321.2 3.0 multiply_reduce_fusion
  324.2 71.3 %spread.3 = (bf16[4096,128]{1,0:T(8,128)(2,1)}, bf16[4096,128]{1,0:T(8,128)(2,1)}, bf16[4096,128]{1,0:T(8,128)(2,1)}) custom-call(bf16[512,1024]{1,0:T(8,128)(2,1)} %fusion.91.query, bf16[512,1024]{1,0:T(8,128)(2,1)} %fusion.90.key, bf16[512,1024]{1,0:T(8,128)(2,1)} %get-tuple-element.356.value), custom_call_target="tpu_custom_call" | custom-call | bytes 1000 | tf_op jit(solution)/shard_map/spread/pallas_call | solution.py:136
  396.8 3.4 collective-permute-start.2
  400.3 3.8 collective-permute-start.3
  404.1 21.6 %attend_own.3 = (bf16[4096,128]{1,0:T(8,128)(2,1)}, f32[4096,128]{1,0:T(8,128)}, f32[4096,128]{1,0:T(8,128)}) custom-call(s32[7]{0:T(128)} %fusion.122.prior, bf16[4096,128]{1,0:T(8,128)(2,1)} %get-tuple-element.125.q_ref.q_seg, bf16[4096,128]{1,0:T(8,128)(2,1)} %get-tuple-element.126.keys, bf16[4096,128]{1,0:T(8,128)(2,1)} %get-tuple-element.127.values, ...), custom_call_target="tpu_custom_call" | custom-call | bytes 1000 | tf_op jit(solution)/shard_map/attend_own/pallas_call | solution.py:737
  425.7 11.1 %collective-permute-done.3.values = bf16[3072,128]{1,0:T(8,128)(2,1)S(1)} collective-permute-done((bf16[3072,128]{1,0:T(8,128)(2,1)S(1)}, bf16[3072,128]{1,0:T(8,128)(2,1)S(1)}, u32[]{:S(2)}, u32[]{:S(2)}) %collective-permute-start.3) | collective-permute-done | bytes 786464 | tf_op jit(solution)/shard_map/ppermute | solution.py:156
  438.6 25.5 %to_rows.3.refs_7_ = bf16[512,1024]{1,0:T(8,128)(2,1)} custom-call(bf16[4096,128]{1,0:T(8,128)(2,1)} %get-tuple-element.131.seg.mixed.out_ref), custom_call_target="tpu_custom_call" | custom-call | bytes 1000 | tf_op jit(solution)/shard_map/to_rows/pallas_call | solution.py:183
  464.1 3.9 multiply_reduce_fusion.7
  469.4 9.2 fusion.21
  479.7 5.0 fusion
  484.7 10.8 multiply_convert_fusion.2
  495.5 5.2 fusion.18
  500.7 3.6 multiply_reduce_fusion.1
  505.7 4.3 fusion.89.refs_0_
  510.0 31.3 %products.2 = (bf16[4096,128]{1,0:T(8,128)(2,1)}, bf16[1024,9472]{1,0:T(8,128)(2,1)}) custom-call(bf16[512,1024]{1,0:T(8,128)(2,1)} %fusion.89.refs_0_, bf16[512,1024]{1,0:T(8,128)(2,1)} %refs_1_, bf16[512,1024]{1,0:T(8,128)(2,1)} %multiply_convert_fusion.4.refs_2_, bf16[512,1024]{1,0:T(8,128)(2,1)} %copy-done.24, ...), custom_call_target="tpu_custom_call" | custom-call | bytes 1000 | tf_op jit(solution)/shard_map/products/pallas_call | solution.py:494
  541.4 2.1 attend_back_halo.2
  544.8 33.7 %attend_back_own.2 = (bf16[4096,128]{1,0:T(8,128)(2,1)}, f32[4096,128]{1,0:T(8,128)}, f32[4096,128]{1,0:T(8,128)}) custom-call(s32[7]{0:T(128)} %fusion.122.prior, bf16[4096,128]{1,0:T(8,128)(2,1)} %get-tuple-element.125.q_ref.q_seg, bf16[4096,128]{1,0:T(8,128)(2,1)} %get-tuple-element.132.grad_seg.grad_ref, ...), custom_call_target="tpu_custom_call" | custom-call | bytes 1000 | tf_op jit(solution)/shard_map/attend_back_own/pallas_call | solution.py:975
  578.5 31.2 %collect_q.2 = (bf16[512,1024]{1,0:T(8,128)(2,1)}, bf16[512,1024]{1,0:T(8,128)(2,1)}) custom-call(bf16[4096,128]{1,0:T(8,128)(2,1)} %get-tuple-element.136.refs_0_, bf16[512,2816]{1,0:T(8,128)(2,1)} %get-tuple-element.308.refs_4_.refs_1_, bf16[3,2816,1024]{2,1,0:T(8,128)(2,1)} %all-gather.13.cloned.1.call-done.refs_2_, f32[512,1024]{1,0:T(8,128)} %copy-done), custom_call_target="tpu_custom_call" | custom-call | bytes 1000 | tf_op jit(solution)/shard_map/collect_q/pallas_call | solution.py:570
  609.7 41.5 %collective-permute-done.4.refs_2_ = bf16[2,3072,128]{2,1,0:T(8,128)(2,1)S(1)} collective-permute-done((bf16[2,3072,128]{2,1,0:T(8,128)(2,1)}, bf16[2,3072,128]{2,1,0:T(8,128)(2,1)S(1)}, u32[]{:S(2)}, u32[]{:S(2)}) %collective-permute-start.4) | collective-permute-done | bytes 1572896 | tf_op jit(solution)/shard_map/ppermute | solution.py:164
  652.4 53.6 %collect_kv.2 = (bf16[512,1024]{1,0:T(8,128)(2,1)}, bf16[512,1024]{1,0:T(8,128)(2,1)}) custom-call(f32[4096,128]{1,0:T(8,128)} %get-tuple-element.141.refs_0_, f32[4096,128]{1,0:T(8,128)} %get-tuple-element.142.refs_1_, bf16[2,3072,128]{2,1,0:T(8,128)(2,1)} %copy-done.34), custom_call_target="tpu_custom_call" | custom-call | bytes 1000 | tf_op jit(solution)/shard_map/collect_kv/pallas_call | solution.py:570
  706.0 3.2 fusion.65
  709.3 3.0 fusion.67
  712.3 3.5 multiply_reduce_fusion.2
  717.4 2.1 fusion.41
  719.5 5.8 convolution_convert_fusion
  725.6 9.8 multiply_convert_fusion.1
  735.4 7.3 fusion.10
  742.8 5.8 multiply_reduce_fusion.3
  751.5 4.2 fusion.101.refs_0_
  755.7 31.3 %products.3 = (bf16[4096,128]{1,0:T(8,128)(2,1)}, bf16[1024,9472]{1,0:T(8,128)(2,1)}) custom-call(bf16[512,1024]{1,0:T(8,128)(2,1)} %fusion.101.refs_0_, bf16[512,1024]{1,0:T(8,128)(2,1)} %copy-done.22, bf16[512,1024]{1,0:T(8,128)(2,1)} %copy-done.23, bf16[512,1024]{1,0:T(8,128)(2,1)} %copy-done.25, bf16[512,2816]{1,0:T(8,128)(2,1)} %copy-done.30, ...), custom_call_target="tpu_custom_call" | custom-call | bytes 1000 | tf_op jit(solution)/shard_map/products/pallas_call | solution.py:494
  787.0 3.8 turn.2
  793.7 2.8 collective-permute-start.6
  798.9 2.5 attend_back_halo.3
  802.8 32.8 %attend_back_own.3 = (bf16[4096,128]{1,0:T(8,128)(2,1)}, f32[4096,128]{1,0:T(8,128)}, f32[4096,128]{1,0:T(8,128)}) custom-call(s32[7]{0:T(128)} %fusion.122.prior, bf16[4096,128]{1,0:T(8,128)(2,1)} %get-tuple-element.111.q_ref.q_seg, bf16[4096,128]{1,0:T(8,128)(2,1)} %get-tuple-element.153.grad_seg.grad_ref, ...), custom_call_target="tpu_custom_call" | custom-call | bytes 1000 | tf_op jit(solution)/shard_map/attend_back_own/pallas_call | solution.py:975
  835.6 35.6 %collect_q.3.dq = bf16[512,1024]{1,0:T(8,128)(2,1)} custom-call(bf16[4096,128]{1,0:T(8,128)(2,1)} %get-tuple-element.159.refs_0_), custom_call_target="tpu_custom_call" | custom-call | bytes 1000 | tf_op jit(solution)/shard_map/collect_q/pallas_call | solution.py:570
  871.2 2.0 fusion.107
  874.9 38.5 %collective-permute-done.5.refs_2_ = bf16[2,3072,128]{2,1,0:T(8,128)(2,1)} collective-permute-done((bf16[2,3072,128]{2,1,0:T(8,128)(2,1)}, bf16[2,3072,128]{2,1,0:T(8,128)(2,1)}, u32[]{:S(2)}, u32[]{:S(2)}) %collective-permute-start.5) | collective-permute-done | bytes 1572896 | tf_op jit(solution)/shard_map/ppermute | solution.py:164
  913.4 50.0 %collect_kv.3 = (bf16[512,1024]{1,0:T(8,128)(2,1)}, bf16[512,1024]{1,0:T(8,128)(2,1)}) custom-call(f32[4096,128]{1,0:T(8,128)} %get-tuple-element.162.refs_0_, f32[4096,128]{1,0:T(8,128)} %get-tuple-element.163.refs_1_, bf16[2,3072,128]{2,1,0:T(8,128)(2,1)} %collective-permute-done.5.refs_2_), custom_call_target="tpu_custom_call" | custom-call | bytes 1000 | tf_op jit(solution)/shard_map/collect_kv/pallas_call | solution.py:570
  965.2 3.2 fusion.54
  968.5 3.0 fusion.50
  971.5 3.6 fusion.36
  977.0 4.5 turn.3
  984.0 80.2 %shed.1 = f32[128,896]{1,0:T(8,128)} custom-call(bf16[512,1024]{1,0:T(8,128)(2,1)} %copy-done.19, bf16[512,1024]{1,0:T(8,128)(2,1)} %collect_q.3.dq, bf16[512,1024]{1,0:T(8,128)(2,1)} %get-tuple-element.175.dk, bf16[512,1024]{1,0:T(8,128)(2,1)} %copy-done.18, f32[1024,128]{1,0:T(8,128)} %pad.9.extra), custom_call_target="tpu_custom_call" | custom-call | bytes 1000 | tf_op jit(solution)/shard_map/shed/pallas_call | solution.py:427
  (252 shorter events, 67.1 us)
Async XLA Ops:
  7.2 5.3 copy-start.65
  7.2 5.3 copy-start.64
  7.2 5.3 copy-start.63
  7.2 5.3 copy-start.62
  7.2 6.0 copy-start.48
  7.2 72.1 %all-gather.7.cloned.1.call-start = ((), (), s32[]{:S(2)}) async-start(), calls=%async_computation.4 | async-start | bytes 2703360 | tf_op jit(solution)/shard_map/all_gather | solution.py:1153
  9.3 180.9 %all-gather.9.cloned.1.call-start = ((), (), s32[]{:S(2)}) async-start(), calls=%async_computation.5 | async-start | bytes 19464192 | tf_op jit(solution)/shard_map/all_gather | solution.py:1161
  82.4 174.5 %all-gather.15.cloned.1.call-start = ((), (), s32[]{:S(2)}) async-start(), calls=%async_computation.12 | async-start | bytes 4014080 | tf_op jit(solution)/shard_map/all_gather | solution.py:1153
  84.6 5.3 copy-start.54
  85.3 4.6 copy-start.50
  85.4 206.2 %copy-start.52 = (f32[1,1024]{1,0:T(1,128)}, f32[1,1024]{1,0:T(1,128)S(1)}, u32[]{:S(2)}) copy-start(f32[1,1024]{1,0:T(1,128)S(1)} %get-tuple-element.333) | copy-start | bytes 12292
  85.7 8.1 copy-start.19
  98.2 82.9 %copy-start.49 = (bf16[256,128]{1,0:T(8,128)(2,1)S(1)}, bf16[256,128]{1,0:T(8,128)(2,1)}, u32[]{:S(2)}) copy-start(bf16[256,128]{1,0:T(8,128)(2,1)} %param.36) | copy-start | bytes 196612
  98.2 82.9 %copy-start.42 = (bf16[704,128]{1,0:T(8,128)(2,1)S(1)}, bf16[704,128]{1,0:T(8,128)(2,1)}, u32[]{:S(2)}) copy-start(bf16[704,128]{1,0:T(8,128)(2,1)} %param.40) | copy-start | bytes 540676
  98.2 82.9 %copy-start.43 = (bf16[128,704]{0,1:T(8,128)(2,1)S(1)}, bf16[128,704]{0,1:T(8,128)(2,1)}, u32[]{:S(2)}) copy-start(bf16[128,704]{0,1:T(8,128)(2,1)} %param.39) | copy-start | bytes 540676
  98.2 82.9 %copy-start.44 = (bf16[128,704]{0,1:T(8,128)(2,1)S(1)}, bf16[128,704]{0,1:T(8,128)(2,1)}, u32[]{:S(2)}) copy-start(bf16[128,704]{0,1:T(8,128)(2,1)} %param.38) | copy-start | bytes 540676
  181.1 11.1 %copy-start.15 = (bf16[4096,128]{1,0:T(8,128)(2,1)S(1)}, bf16[4096,128]{1,0:T(8,128)(2,1)}, u32[]{:S(2)}) copy-start(bf16[4096,128]{1,0:T(8,128)(2,1)} %get-tuple-element.112.keys) | copy-start | bytes 3145732
  182.1 14.6 %copy-start.16 = (bf16[4096,128]{1,0:T(8,128)(2,1)S(1)}, bf16[4096,128]{1,0:T(8,128)(2,1)}, u32[]{:S(2)}) copy-start(bf16[4096,128]{1,0:T(8,128)(2,1)} %get-tuple-element.113.values) | copy-start | bytes 3145732
  192.2 7.8 copy-start.66
  192.2 122.1 %all-gather.11.cloned.1.call-start = ((), (), s32[]{:S(2)}) async-start(), calls=%async_computation.6 | async-start | bytes 9437184 | tf_op jit(solution)/shard_map/all_gather | solution.py:1161
  193.2 28.6 %collective-permute-start = (bf16[3072,128]{1,0:T(8,128)(2,1)}, bf16[3072,128]{1,0:T(8,128)(2,1)S(1)}, u32[]{:S(2)}, u32[]{:S(2)}) collective-permute-start(bf16[3072,128]{1,0:T(8,128)(2,1)} %slice.181), channel_id=1, source_target_pairs={{0,8},{4,12},{8,16},{12,20},{16,24},{20,28},{1,9},{5,13},{9,17},{1... | collective-permute-start | bytes 2359304 | tf_op jit(solution)/shard_map/ppermute | solution.py:156
  197.6 33.4 %collective-permute-start.1 = (bf16[3072,128]{1,0:T(8,128)(2,1)}, bf16[3072,128]{1,0:T(8,128)(2,1)S(1)}, u32[]{:S(2)}, u32[]{:S(2)}) collective-permute-start(bf16[3072,128]{1,0:T(8,128)(2,1)} %slice.182), channel_id=1, source_target_pairs={{0,8},{4,12},{8,16},{12,20},{16,24},{20,28},{1,9},{5,13},{9,17},{1... | collective-permute-start | bytes 2359304 | tf_op jit(solution)/shard_map/ppermute | solution.py:156
  221.8 9.1 copy-start.26
  259.3 210.1 %all-gather.13.cloned.1.call-start = ((), (), s32[]{:S(2)}) async-start(), calls=%async_computation.7 | async-start | bytes 19464192 | tf_op jit(solution)/shard_map/all_gather | solution.py:1161
  262.6 493.0 %reduce-scatter.5.cloned.1.call-start = ((), (), s32[]{:S(2)}) async-start(), calls=%async_computation.8 | async-start | bytes 21823488 | tf_op jit(solution)/shard_map/reduce_scatter | solution.py:1341
  291.0 18.4 %copy-start.10 = (f32[512,1024]{1,0:T(8,128)}, f32[512,1024]{1,0:T(8,128)S(1)}, u32[]{:S(2)}) copy-start(f32[512,1024]{1,0:T(8,128)S(1)} %get-tuple-element.342) | copy-start | bytes 6291460
  292.2 8.0 copy-start.23
  292.2 17.2 %slice-start = ((s8[17301504]{0:T(1024)(128)(4,1)}), s8[4194304]{0:T(1024)(128)(4,1)S(1)}, s32[]{:S(2)}) async-start(s8[17301504]{0:T(1024)(128)(4,1)} %bitcast.314), calls=%async_computation.13 | async-start | bytes 8388608
  292.2 17.2 %slice-start.1 = ((s8[17301504]{0:T(1024)(128)(4,1)}), s8[4194304]{0:T(1024)(128)(4,1)S(1)}, s32[]{:S(2)}) async-start(s8[17301504]{0:T(1024)(128)(4,1)} %bitcast.314), calls=%async_computation.14 | async-start | bytes 8388608
  300.2 9.2 slice-start.2
  300.2 9.2 slice-start.3
  300.2 9.2 slice-start.4
  309.4 3.3 copy-start.30
  314.3 6.9 copy-start.39
  314.3 4.6 copy-start.41
  395.5 4.7 copy-start.17
  396.8 28.9 %collective-permute-start.2 = (bf16[3072,128]{1,0:T(8,128)(2,1)S(1)}, bf16[3072,128]{1,0:T(8,128)(2,1)S(1)}, u32[]{:S(2)}, u32[]{:S(2)}) collective-permute-start(bf16[3072,128]{1,0:T(8,128)(2,1)S(1)} %slice.195), channel_id=1, source_target_pairs={{0,8},{4,12},{8,16},{12,20},{16,24},{20,28},{1,9},{5,13},{9,17},{1... | collective-permute-start | bytes 2359304 | tf_op jit(solution)/shard_map/ppermute | solution.py:156
  400.3 36.5 %collective-permute-start.3 = (bf16[3072,128]{1,0:T(8,128)(2,1)S(1)}, bf16[3072,128]{1,0:T(8,128)(2,1)S(1)}, u32[]{:S(2)}, u32[]{:S(2)}) collective-permute-start(bf16[3072,128]{1,0:T(8,128)(2,1)S(1)} %slice.196), channel_id=1, source_target_pairs={{0,8},{4,12},{8,16},{12,20},{16,24},{20,28},{1,9},{5,13},{9,17},{1... | collective-permute-start | bytes 2359304 | tf_op jit(solution)/shard_map/ppermute | solution.py:156
  425.7 11.1 %copy-start.28 = (bf16[3072,128]{1,0:T(8,128)(2,1)}, bf16[3072,128]{1,0:T(8,128)(2,1)S(1)}, u32[]{:S(2)}) copy-start(bf16[3072,128]{1,0:T(8,128)(2,1)S(1)} %collective-permute-done.2.keys) | copy-start | bytes 2359300
  468.0 36.3 %copy-start = (f32[512,1024]{1,0:T(8,128)}, f32[512,1024]{1,0:T(8,128)S(1)}, u32[]{:S(2)}) copy-start(f32[512,1024]{1,0:T(8,128)S(1)} %get-tuple-element.348.refs_3_) | copy-start | bytes 6291460
  469.4 9.2 copy-start.8
  469.4 10.3 copy-start.4
  495.5 5.2 copy-start.33
  505.7 4.3 copy-start.24
  541.4 294.3 %reduce-scatter.7.cloned.1.call-start = ((), (), s32[]{:S(2)}) async-start(), calls=%async_computation.9 | async-start | bytes 7077888 | tf_op jit(solution)/shard_map/reduce_scatter | solution.py:1353
  543.5 107.7 %collective-permute-start.4 = (bf16[2,3072,128]{2,1,0:T(8,128)(2,1)}, bf16[2,3072,128]{2,1,0:T(8,128)(2,1)S(1)}, u32[]{:S(2)}, u32[]{:S(2)}) collective-permute-start(bf16[2,3072,128]{2,1,0:T(8,128)(2,1)} %get-tuple-element.139), channel_id=1, source_target_pairs={{8,0},{12,4},{16,8},{20,12},{24,16},{28,20},{9,1},{13,5},{17,9},{2... | collective-permute-start | bytes 4718600 | tf_op jit(solution)/shard_map/ppermute | solution.py:164
  712.3 3.8 copy-start.9
  712.3 3.8 copy-start.13
  725.4 251.6 %reduce-scatter.9.cloned.1.call-start = ((), (), s32[]{:S(2)}) async-start(), calls=%async_computation.10 | async-start | bytes 21823488 | tf_op jit(solution)/shard_map/reduce_scatter | solution.py:1369
  725.6 9.8 copy-start.22
  735.4 7.3 copy-start.32
  735.4 7.3 copy-start.31
  735.4 7.3 copy-start.11
  735.4 7.3 copy-start.53
  735.4 7.3 copy-start.59
  742.7 5.8 copy-start.61
  790.8 278.2 %reduce-scatter.11.cloned.1.call-start = ((), (), s32[]{:S(2)}) async-start(), calls=%async_computation.11 | async-start | bytes 4014080 | tf_op jit(solution)/shard_map/reduce_scatter | solution.py:1199
  793.7 77.5 %collective-permute-start.6 = (bf16[2368,128]{1,0:T(8,128)(2,1)}, bf16[2368,128]{1,0:T(8,128)(2,1)}, u32[]{:S(2)}, u32[]{:S(2)}) collective-permute-start(bf16[2368,128]{1,0:T(8,128)(2,1)} %get-tuple-element.311), channel_id=1, source_target_pairs={{0,1},{1,2},{2,3},{3,0},{4,5},{5,6},{6,7},{7,4},{8,9},{9,10},{10,1... | collective-permute-start | bytes 1818632 | tf_op jit(solution)/shard_map/ppermute | solution.py:1216
  796.6 74.7 %collective-permute-start.7 = (bf16[2368,128]{1,0:T(8,128)(2,1)}, bf16[2368,128]{1,0:T(8,128)(2,1)}, u32[]{:S(2)}, u32[]{:S(2)}) collective-permute-start(bf16[2368,128]{1,0:T(8,128)(2,1)} %get-tuple-element.313), channel_id=1, source_target_pairs={{0,2},{1,3},{2,0},{3,1},{4,6},{5,7},{6,4},{7,5},{8,10},{9,11},{10,... | collective-permute-start | bytes 1818632 | tf_op jit(solution)/shard_map/ppermute | solution.py:1216
  798.3 72.9 %collective-permute-start.8 = (bf16[2368,128]{1,0:T(8,128)(2,1)}, bf16[2368,128]{1,0:T(8,128)(2,1)}, u32[]{:S(2)}, u32[]{:S(2)}) collective-permute-start(bf16[2368,128]{1,0:T(8,128)(2,1)} %get-tuple-element.312), channel_id=1, source_target_pairs={{0,3},{1,0},{2,1},{3,2},{4,7},{5,4},{6,5},{7,6},{8,11},{9,8},{10,9... | collective-permute-start | bytes 1818632 | tf_op jit(solution)/shard_map/ppermute | solution.py:1216
  801.5 111.9 %collective-permute-start.5 = (bf16[2,3072,128]{2,1,0:T(8,128)(2,1)}, bf16[2,3072,128]{2,1,0:T(8,128)(2,1)}, u32[]{:S(2)}, u32[]{:S(2)}) collective-permute-start(bf16[2,3072,128]{2,1,0:T(8,128)(2,1)} %get-tuple-element.160), channel_id=1, source_target_pairs={{8,0},{12,4},{16,8},{20,12},{24,16},{28,20},{9,1},{13,5},{17,9},{2... | collective-permute-start | bytes 4718600 | tf_op jit(solution)/shard_map/ppermute | solution.py:164
  971.5 3.6 copy-start.57
  971.5 3.6 copy-start.14
  1070.2 4.0 copy-start.38
  (27 other events, 49.5 us)
Sparse Core Ops, SparseCore 0:
  10.2 69.0 all-gather.6
  82.5 107.6 all-gather.8
  192.3 64.5 all-gather.14
  259.4 54.5 all-gather.10
  315.8 95.9 all-gather.12
  541.5 176.2 reduce-scatter.4
  725.5 76.1 reduce-scatter.6
  805.3 161.8 reduce-scatter.8
  981.7 82.6 reduce-scatter.10
